TPU v7x, 32 devices: a whole 2x2x4 slice. The times are simulated.
32 devices in a mesh: groups: 2 (over x), row: 8 (over z, y), col: 2 (over core).
Axes of the slice: x: 2, y: 2, z: 4, core: 2. Of those that a mesh axis runs over, the one named last changes fastest.
Arguments:
- tokens: bfloat16 [1024, 8192], P(('groups', 'row'), 'col'), parts along dimension 0, may hold values from -6 to 6
- gate_weight: bfloat16 [8192, 14336], P('col', 'row'), may hold values from -0.125 to 0.125
- up_weight: bfloat16 [8192, 14336], P('col', 'row'), may hold values from -0.125 to 0.125
- down_weight: bfloat16 [14336, 8192], P('row', 'col'), may hold values from -0.09375 to 0.09375
- gate_mask: int32 [64, 112], P('col', 'row'), may hold values from 0 to 1, as said below
- up_mask: int32 [64, 112], P('col', 'row'), may hold values from 0 to 1, as said below
- down_mask: int32 [112, 64], P('row', 'col'), may hold values from 0 to 1, as said below
Outputs:
- mixed: bfloat16 [1024, 8192], P(('groups', 'row'), 'col'), parts along dimension 0
There are 2 independent parts, one for each index of `groups`. A program takes and returns all parts, laid end to end along the dimension named above; an argument that names none is the same for every part. Nothing has to cross between parts.
Inputs may be any that keep to these rules, and one draw needn't show every extreme that they name: `gate_mask`: 1 keeps the 128 x 128 block of the matching projection, 0 prunes it. `up_mask`: 1 keeps the 128 x 128 block of the matching projection, 0 prunes it. `down_mask`: 1 keeps the 128 x 128 block of the matching projection, 0 prunes it.
All inputs are finite; a program needn't handle non-finite values.
Results may differ from a plain program's by a relative error of at most 0.0049.
Values may be sent and summed in bfloat16 or wider, within the bound.
No kernel may reach another device: no remote copies, remote signals or barrier semaphores. Data moves between devices by JAX's collectives and lax.ppermute only.
A program may use at most 192 MiB of HBM per device.

v0:
```python
import functools

import jax
import jax.numpy as jnp
from jax import lax
from jax.experimental import pallas as pl
from jax.experimental.pallas import tpu as pltpu
from jax.sharding import PartitionSpec as P

SIDE = 128
DEPTH = 2
ITEMS = 8
AHEAD = 8
SLOTS = AHEAD + 1
F32 = jnp.float32
BF16 = jnp.bfloat16


def round_up(n, unit):
    return -(-n // unit) * unit


def kept_items(mask):
    deep, wide = mask.shape
    kept = (mask != 0).astype(jnp.int32).T
    row = jnp.arange(deep)
    before = jnp.sum(jnp.where(row[None, :, None] > row[None, None, :], kept[:, None, :], 0), axis=2)
    filled = round_up(jnp.sum(kept, axis=1), DEPTH)
    column = jnp.arange(wide)
    ends = jnp.sum(jnp.where(column[:, None] >= column[None, :], filled[None, :], 0), axis=1)
    place = jnp.where(kept != 0, (ends - filled)[:, None] + before, -1)
    spots = jnp.arange(round_up(wide * round_up(deep, DEPTH), DEPTH * ITEMS))
    rows = deep + jnp.sum(
        jnp.where(place[None] == spots[:, None, None], row[None, None, :] - deep, 0), axis=(1, 2)
    )
    items = jnp.arange(spots.shape[0] // DEPTH + 1)
    columns = jnp.sum((ends[None, :] <= items[:, None] * DEPTH).astype(jnp.int32), axis=1)
    trips = round_up(jnp.max(ends[None, :] + items[:, None], axis=1) - items, DEPTH * ITEMS) // (DEPTH * ITEMS)
    columns = jnp.where(items == items.shape[0] - 1, trips, jnp.minimum(columns, wide - 1))
    return rows.astype(jnp.int32), columns.astype(jnp.int32)


def trips_of(columns):
    return columns[columns.shape[0] - 1]


def block_of(i):
    return pl.ds(pl.multiple_of(i * SIDE, SIDE), SIDE)


def start_fetches(k, rows, columns, weight, fetched, sems):
    deep = weight.shape[0] // SIDE
    slot = lax.rem(k, SLOTS)
    for t in range(ITEMS):
        item = k * ITEMS + t
        column = columns[item]
        for d in range(DEPTH):
            i = rows[item * DEPTH + d]
            i = jnp.where(i == deep, 0, i)
            pltpu.make_async_copy(
                weight.at[block_of(i), block_of(column)],
                fetched.at[slot, pl.ds((t * DEPTH + d) * SIDE, SIDE), :],
                sems.at[slot],
            ).start()


def first_fetches(rows, columns, weight, fetched, sems):
    lax.fori_loop(
        0,
        jnp.minimum(AHEAD, trips_of(columns)),
        lambda k, _: (start_fetches(k, rows, columns, weight, fetched, sems), 0)[1],
        0,
    )


def multiply_trip(k, rows, columns, held, blocks, total):
    deep = DEPTH * SIDE
    for t in range(ITEMS):
        item = k * ITEMS + t
        lhs = jnp.concatenate([held[:, block_of(rows[item * DEPTH + d])] for d in range(DEPTH)], axis=1)
        rhs = blocks[pl.ds(t * deep, deep), :]
        total[:, block_of(columns[item])] += jnp.dot(lhs, rhs, preferred_element_type=F32)


def multiply(rows, columns, weight, held, fetched, sems, total):
    def trip(k, _, more):
        slot = lax.rem(k, SLOTS)
        pltpu.make_async_copy(fetched.at[slot], fetched.at[slot], sems.at[slot]).wait()
        multiply_trip(k, rows, columns, held, fetched.at[slot], total)
        if more:
            start_fetches(k + AHEAD, rows, columns, weight, fetched, sems)
        return 0

    trips = trips_of(columns)
    last = jnp.maximum(trips - AHEAD, 0)
    lax.fori_loop(0, last, functools.partial(trip, more=True), 0)
    lax.fori_loop(last, trips, functools.partial(trip, more=False), 0)


FETCH_SCRATCH = [pltpu.VMEM((SLOTS, ITEMS * DEPTH * SIDE, SIDE), BF16), pltpu.SemaphoreType.DMA((SLOTS,))]


SMEM = pl.BlockSpec(memory_space=pltpu.SMEM)
VMEM = pl.BlockSpec(memory_space=pltpu.VMEM)
HBM = pl.BlockSpec(memory_space=pltpu.HBM)


def pack_kernel(*refs):
    lists, (gate, up, gate_packed, up_packed, sems) = refs[:4], refs[4:]
    jobs = [(*lists[2 * w : 2 * w + 2], *ends) for w, ends in enumerate(((gate, gate_packed), (up, up_packed)))]

    def start(k, _, w, rows, columns, weight, packed):
        deep = weight.shape[0] // SIDE
        for t in range(ITEMS * DEPTH):
            place = k * ITEMS * DEPTH + t
            i = rows[place]
            pltpu.make_async_copy(
                weight.at[block_of(jnp.where(i == deep, 0, i)), block_of(columns[k * ITEMS + t // DEPTH])],
                packed.at[block_of(place), :],
                sems.at[w],
            ).start()
        return 0

    def wait(k, _, w, packed):
        span = ITEMS * DEPTH * SIDE
        here = packed.at[pl.ds(pl.multiple_of(k * span, span), span), :]
        pltpu.make_async_copy(here, here, sems.at[w]).wait()
        return 0

    for w, (rows, columns, weight, packed) in enumerate(jobs):
        lax.fori_loop(
            0, trips_of(columns), functools.partial(start, w=w, rows=rows, columns=columns, weight=weight, packed=packed), 0
        )
    for w, (_, columns, _, packed) in enumerate(jobs):
        lax.fori_loop(0, trips_of(columns), functools.partial(wait, w=w, packed=packed), 0)


def pack(gate_items, up_items, gate, up):
    return pl.pallas_call(
        pack_kernel,
        out_shape=[jax.ShapeDtypeStruct((items[0].shape[0] * SIDE, SIDE), BF16) for items in (gate_items, up_items)],
        in_specs=[SMEM] * 4 + [HBM] * 2,
        out_specs=[VMEM] * 2,
        scratch_shapes=[pltpu.SemaphoreType.DMA((2,))],
        compiler_params=pltpu.CompilerParams(vmem_limit_bytes=1 << 20),
        cost_estimate=pl.CostEstimate(flops=0, bytes_accessed=2 * gate.size, transcendentals=0),
    )(*gate_items, *up_items, gate, up)


def tokens_kernel(places, *refs):
    lists, refs = refs[:4], refs[4:]
    pieces = refs[: len(places)]
    gate, up, out, held, sems = refs[len(places) :]
    deep = held.shape[1] - SIDE
    width = out.shape[1] // 2
    copies = [
        pltpu.make_async_copy(piece, held.at[pl.ds(row, piece.shape[0]), pl.ds(column, piece.shape[1])], sems.at[k])
        for k, (piece, (row, column)) in enumerate(zip(pieces, places))
    ]
    for copy in copies:
        copy.start()
    held[:, deep:] = jnp.zeros((held.shape[0], SIDE), BF16)
    out[...] = jnp.zeros(out.shape, F32)
    for copy in copies:
        copy.wait()
    span = ITEMS * DEPTH * SIDE
    for w, packed in enumerate((gate, up)):
        rows, columns = lists[2 * w : 2 * w + 2]

        def trip(k, _, rows=rows, columns=columns, packed=packed, w=w):
            blocks = packed.at[pl.ds(pl.multiple_of(k * span, span), span), :]
            multiply_trip(k, rows, columns, held, blocks, out.at[:, pl.ds(w * width, width)])
            return 0

        lax.fori_loop(0, trips_of(columns), trip, 0)


def tokens_product(gate_items, up_items, pieces, places, gate, up, deep, width):
    rows = max(row + piece.shape[0] for piece, (row, _) in zip(pieces, places))
    return pl.pallas_call(
        functools.partial(tokens_kernel, places),
        out_shape=jax.ShapeDtypeStruct((rows, 2 * width), F32),
        in_specs=[SMEM] * 4 + [VMEM] * (len(pieces) + 2),
        out_specs=VMEM,
        scratch_shapes=[pltpu.VMEM((rows, deep + SIDE), BF16), pltpu.SemaphoreType.DMA((len(pieces),))],
        compiler_params=pltpu.CompilerParams(vmem_limit_bytes=6 << 20),
        cost_estimate=pl.CostEstimate(
            flops=16 * rows * deep * width, bytes_accessed=16 * deep * width, transcendentals=0
        ),
    )(*gate_items, *up_items, *pieces, gate, up)


def down_kernel(groups, opposite, rows, columns, *refs):
    sums, refs = refs[: 2 * groups], refs[2 * groups :]
    down, refs = refs[0], refs[1:]
    if opposite:
        on, back, total, held, fetched, sems = refs
    else:
        total, held, fetched, sems = refs
    first_fetches(rows, columns, down, fetched, sems)
    deep = down.shape[0]
    held[:, deep:] = jnp.zeros((held.shape[0], SIDE), BF16)
    total[...] = jnp.zeros(total.shape, F32)
    at = 0
    for g in range(groups):
        mine, other = sums[2 * g : 2 * g + 2]

        def some(s, _, at=at, mine=mine, other=other):
            here = pl.ds(pl.multiple_of(s * 16, 16), 16)
            value = mine[here, :] + other[here, :]
            silu = value[:, :deep] / (1.0 + jnp.exp(-value[:, :deep]))
            held[pl.ds(pl.multiple_of(at + s * 16, 16), 16), pl.ds(0, deep)] = (silu * value[:, deep:]).astype(BF16)
            return 0

        lax.fori_loop(0, mine.shape[0] // 16, some, 0)
        at += mine.shape[0]
    multiply(rows, columns, down, held, fetched, sems, total)
    if opposite:
        half = on.shape[1]
        on[...] = total[:, pl.ds(0, half)].astype(BF16)
        back[...] = total[:, pl.ds(half, half)].astype(BF16)


def down_product(items, sums, down, opposite):
    deep, width = down.shape
    groups = len(sums)
    rows = sum(mine.shape[0] for mine, _ in sums)
    whole = pltpu.VMEM((rows, width), F32)
    half = jax.ShapeDtypeStruct((rows, width // 2), BF16)
    return pl.pallas_call(
        functools.partial(down_kernel, groups, opposite),
        out_shape=(half, half) if opposite else jax.ShapeDtypeStruct((rows, width), F32),
        in_specs=[SMEM] * 2 + [VMEM] * (2 * groups) + [HBM],
        out_specs=(VMEM, VMEM) if opposite else VMEM,
        scratch_shapes=([whole] if opposite else [])
        + [pltpu.VMEM((rows, deep + SIDE), BF16)]
        + FETCH_SCRATCH,
        compiler_params=pltpu.CompilerParams(vmem_limit_bytes=14 << 20),
        cost_estimate=pl.CostEstimate(
            flops=rows * deep * width * 2, bytes_accessed=deep * width * 2, transcendentals=rows * deep
        ),
    )(*items, *(part for pair in sums for part in pair), down)


def ring_of(n):
    order = list(range(n)) if n > 8 else list(range(0, n, 2)) + list(range(n - 1, 0, -2))
    onward = [(order[k], order[(k + 1) % n]) for k in range(n)]
    return onward, [(b, a) for a, b in onward]


def tie(values, *before):
    return lax.optimization_barrier((values, before))[0]


def scatter(parts, onward, back, n):
    far = n // 2
    on, ba = parts[far]
    half = on.shape[1]
    for k in range(far, 0, -1):
        on, ba = lax.ppermute(on, "row", onward).astype(F32), lax.ppermute(ba, "row", back).astype(F32)
        if k == 1:
            return (parts[0][0] + on + ba).astype(BF16)
        behind, ahead = parts[k - 1]
        if k == far:
            on = jnp.concatenate((ahead[:, :half] + on, ahead[:, half:]), axis=1)
            ba = jnp.concatenate((behind[:, :half], behind[:, half:] + ba), axis=1)
        else:
            on, ba = ahead + on, behind + ba
        on, ba = tie((on.astype(BF16), ba.astype(BF16)))


def body(n, tokens, gate, up, down, gate_mask, up_mask, down_mask):
    onward, back = ring_of(n)
    swap = [(0, 1), (1, 0)]
    far = n // 2
    half = tokens.shape[1] // 2
    gate_items, up_items, down_items = kept_items(gate_mask), kept_items(up_mask), kept_items(down_mask)
    rows = tokens.shape[0]
    def product(group):
        pieces, places = [], []
        at = 0
        for k in group:
            for piece in steps[k]:
                pieces.append(piece)
                places.append((at, 0))
                at += rows
        if group[-1] == far:
            places[-2:] = [(at - 2 * rows, 0), (at - 2 * rows, half)]
        mine = tokens_product(gate_items, up_items, pieces, places, *packed, *gate.shape)
        return mine, lax.ppermute(mine, "col", swap)

    gate, up, down = (pltpu.with_memory_space_constraint(w, pltpu.HBM) for w in (gate, up, down))
    packed = pack(gate_items, up_items, gate, up)
    behind = ahead = tokens
    steps = [(tokens,)]
    sums = []
    for k in range(1, far + 1):
        if k > 2:
            sums.append(product((0, 1) if k == 3 else (k - 2,)))
            behind, ahead = tie((behind, ahead), sums[-1][0])
        if k == far:
            behind, ahead = behind[:, :half], ahead[:, half:]
        behind, ahead = lax.ppermute(behind, "row", onward), lax.ppermute(ahead, "row", back)
        steps.append((behind, ahead))
    sums += [product((far - 1,)), product((far,))]
    parts = [None] * (far + 1)
    parts[far] = down_product(down_items, sums[-1:], down, True)
    late = down_product(down_items, sums[-2:-1], down, False)
    early = down_product(down_items, sums[:-2], down, False)
    parts[0] = (early[:rows],)
    for k in range(1, far):
        source, at = (late, 0) if k == far - 1 else (early, (2 * k - 1) * rows)
        parts[k] = (source[at : at + rows], source[at + rows : at + 2 * rows])
    return scatter(parts, onward, back, n)


def solution(mesh):
    return jax.shard_map(
        functools.partial(body, mesh.shape["row"]),
        mesh=mesh,
        in_specs=(
            P(("groups", "row"), "col"),
            P("col", "row"),
            P("col", "row"),
            P("row", "col"),
            P("col", "row"),
            P("col", "row"),
            P("row", "col"),
        ),
        out_specs=P(("groups", "row"), "col"),
        check_vma=False,
    )
```

profile of v0, /device:TPU:0, one launch (start us, length us, event | category | flops | bytes accessed | tf_op | source)
XLA Modules:
  0.0 113.6 jit_solution(10624499328753871011)
XLA Ops:
  0.0 3.0 %collective-permute-start = (bf16[64,4096]{1,0:T(8,128)(2,1)}, bf16[64,4096]{1,0:T(8,128)(2,1)S(1)}, u32[]{:S(2)}, u32[]{:S(2)}) collective-permute-start(bf16[64,4096]{1,0:T(8,128)(2,1)} %refs_4_.4), channel_id=1, source_target_pairs={{0,4},{4,8},{8,12},{12,14},{14,10},{10,6},{6,2},{2,0},{1,5},{5,9},... | collective-permute-start | bytes 1572872 | tf_op jit(solution)/shard_map/ppermute | solution.py:303
  3.1 0.8 convert_reduce_fusion.3
  3.9 0.8 convert_reduce_fusion.4
  4.7 0.1 select_reduce_fusion.7
  4.9 0.1 select_reduce_fusion.8
  5.0 0.5 select_reduce_fusion.3
  5.5 0.1 add_select_fusion
  5.6 0.3 select_reduce_fusion
  5.9 0.1 convert_reduce_fusion.1
  6.0 0.7 convert_reduce_fusion.5
  6.8 0.1 select_reduce_fusion.6
  6.9 0.0 copy-start
  6.9 4.0 %shard_map.73 = (bf16[57344,128]{1,0:T(8,128)(2,1)S(1)}, bf16[57344,128]{1,0:T(8,128)(2,1)S(1)}) custom-call(s32[448]{0:T(512)S(1)} %broadcast_add_fusion.1.refs_0_, s32[225]{0:T(256)S(1)} %get-tuple-element.60.refs_1_, s32[448]{0:T(512)S(1)} %broadcast_add_fusion.refs_2_, s32[225]{0:T(256)S(1)} %get-tuple-element.59.refs_3_, bf16[4096,1792]{1,0:T(8,128)(2,1)} %refs_4_.3, ...), custom_call_target="tpu_custom_call" | custom-call | bytes 14680064 | tf_op jit(solution)/shard_map/pallas_call | solution.py:139
  11.0 4.1 %collective-permute-done.refs_5_ = bf16[64,4096]{1,0:T(8,128)(2,1)S(1)} collective-permute-done((bf16[64,4096]{1,0:T(8,128)(2,1)}, bf16[64,4096]{1,0:T(8,128)(2,1)S(1)}, u32[]{:S(2)}, u32[]{:S(2)}) %collective-permute-start) | collective-permute-done | bytes 524320 | tf_op jit(solution)/shard_map/ppermute | solution.py:303
  15.1 1.8 %collective-permute-start.3 = (bf16[64,4096]{1,0:T(8,128)(2,1)S(1)}, bf16[64,4096]{1,0:T(8,128)(2,1)S(1)}, u32[]{:S(2)}, u32[]{:S(2)}) collective-permute-start(bf16[64,4096]{1,0:T(8,128)(2,1)S(1)} %collective-permute-done.refs_5_), channel_id=1, source_target_pairs={{0,4},{4,8},{8,12},{12,14},{14,10},{10,6},{6,2},{2,0},{1,5},{5,9},... | collective-permute-start | bytes 1572872 | tf_op jit(solution)/shard_map/ppermute | solution.py:303
  16.9 0.0 collective-permute-done.1.refs_6_
  16.9 0.2 collective-permute-start.4
  17.1 6.4 %shard_map.74.refs_0_ = f32[192,3584]{1,0:T(8,128)S(1)} custom-call(s32[448]{0:T(512)S(1)} %broadcast_add_fusion.1.refs_0_, s32[225]{0:T(256)S(1)} %get-tuple-element.60.refs_1_, s32[448]{0:T(512)S(1)} %broadcast_add_fusion.refs_2_, s32[225]{0:T(256)S(1)} %get-tuple-element.59.refs_3_, bf16[64,4096]{1,0:T(8,128)(2,1)S(1)} %copy-done, ...), custom_call_target="tpu_custom_call" | custom-call | flops 22548578304 | bytes 117440512 | tf_op jit(solution)/shard_map/pallas_call | solution.py:180
  23.6 4.7 %collective-permute-done.3.refs_4_ = bf16[64,4096]{1,0:T(8,128)(2,1)S(1)} collective-permute-done((bf16[64,4096]{1,0:T(8,128)(2,1)S(1)}, bf16[64,4096]{1,0:T(8,128)(2,1)S(1)}, u32[]{:S(2)}, u32[]{:S(2)}) %collective-permute-start.3) | collective-permute-done | bytes 524320 | tf_op jit(solution)/shard_map/ppermute | solution.py:303
  28.2 1.2 %collective-permute-done.4.refs_5_ = bf16[64,4096]{1,0:T(8,128)(2,1)S(1)} collective-permute-done((bf16[64,4096]{1,0:T(8,128)(2,1)S(1)}, bf16[64,4096]{1,0:T(8,128)(2,1)S(1)}, u32[]{:S(2)}, u32[]{:S(2)}) %collective-permute-start.4) | collective-permute-done | bytes 524320 | tf_op jit(solution)/shard_map/ppermute | solution.py:303
  29.4 1.6 %collective-permute-start.6 = (bf16[64,4096]{1,0:T(8,128)(2,1)S(1)}, bf16[64,4096]{1,0:T(8,128)(2,1)S(1)}, u32[]{:S(2)}, u32[]{:S(2)}) collective-permute-start(bf16[64,4096]{1,0:T(8,128)(2,1)S(1)} %collective-permute-done.3.refs_4_), channel_id=1, source_target_pairs={{0,4},{4,8},{8,12},{12,14},{14,10},{10,6},{6,2},{2,0},{1,5},{5,9},... | collective-permute-start | bytes 1572872 | tf_op jit(solution)/shard_map/ppermute | solution.py:303
  31.0 0.4 collective-permute-start.7
  31.4 5.2 %shard_map.75.refs_2_ = f32[128,3584]{1,0:T(8,128)S(1)} custom-call(s32[448]{0:T(512)S(1)} %broadcast_add_fusion.1.refs_0_, s32[225]{0:T(256)S(1)} %get-tuple-element.60.refs_1_, s32[448]{0:T(512)S(1)} %broadcast_add_fusion.refs_2_, s32[225]{0:T(256)S(1)} %get-tuple-element.59.refs_3_, bf16[64,4096]{1,0:T(8,128)(2,1)S(1)} %collective-permute-done.3.refs_4_, ...), custom_call_target="tpu_custom_call" | custom-call | flops 15032385536 | bytes 117440512 | tf_op jit(solution)/shard_map/pallas_call | solution.py:180
  36.7 4.3 %collective-permute-done.6.refs_4_ = bf16[64,4096]{1,0:T(8,128)(2,1)S(1)} collective-permute-done((bf16[64,4096]{1,0:T(8,128)(2,1)S(1)}, bf16[64,4096]{1,0:T(8,128)(2,1)S(1)}, u32[]{:S(2)}, u32[]{:S(2)}) %collective-permute-start.6) | collective-permute-done | bytes 524320 | tf_op jit(solution)/shard_map/ppermute | solution.py:303
  41.0 2.0 %collective-permute-done.7.refs_5_ = bf16[64,4096]{1,0:T(8,128)(2,1)S(1)} collective-permute-done((bf16[64,4096]{1,0:T(8,128)(2,1)S(1)}, bf16[64,4096]{1,0:T(8,128)(2,1)S(1)}, u32[]{:S(2)}, u32[]{:S(2)}) %collective-permute-start.7) | collective-permute-done | bytes 524320 | tf_op jit(solution)/shard_map/ppermute | solution.py:303
  43.0 0.5 collective-permute-start.10
  43.6 1.6 %collective-permute-start.9 = (bf16[64,2048]{1,0:T(8,128)(2,1)S(1)}, bf16[64,2048]{1,0:T(8,128)(2,1)S(1)}, u32[]{:S(2)}, u32[]{:S(2)}) collective-permute-start(bf16[64,2048]{1,0:T(8,128)(2,1)S(1)} %slice.45), channel_id=1, source_target_pairs={{0,4},{4,8},{8,12},{12,14},{14,10},{10,6},{6,2},{2,0},{1,5},{5,9},... | collective-permute-start | bytes 786440 | tf_op jit(solution)/shard_map/ppermute | solution.py:303
  45.2 5.2 %shard_map.77.refs_0_ = f32[128,3584]{1,0:T(8,128)S(1)} custom-call(s32[448]{0:T(512)S(1)} %broadcast_add_fusion.1.refs_0_, s32[225]{0:T(256)S(1)} %get-tuple-element.60.refs_1_, s32[448]{0:T(512)S(1)} %broadcast_add_fusion.refs_2_, s32[225]{0:T(256)S(1)} %get-tuple-element.59.refs_3_, bf16[64,4096]{1,0:T(8,128)(2,1)S(1)} %collective-permute-done.6.refs_4_, ...), custom_call_target="tpu_custom_call" | custom-call | flops 15032385536 | bytes 117440512 | tf_op jit(solution)/shard_map/pallas_call | solution.py:180
  50.4 0.1 collective-permute-start.8
  50.5 0.1 select_reduce_fusion.5
  50.6 0.0 collective-permute-done.10.refs_5_
  50.6 4.2 %shard_map.79.refs_0_ = f32[64,3584]{1,0:T(8,128)S(1)} custom-call(s32[448]{0:T(512)S(1)} %broadcast_add_fusion.1.refs_0_, s32[225]{0:T(256)S(1)} %get-tuple-element.60.refs_1_, s32[448]{0:T(512)S(1)} %broadcast_add_fusion.refs_2_, s32[225]{0:T(256)S(1)} %get-tuple-element.59.refs_3_, bf16[64,2048]{1,0:T(8,128)(2,1)S(1)} %collective-permute-done.9.refs_4_, ...), custom_call_target="tpu_custom_call" | custom-call | flops 7516192768 | bytes 117440512 | tf_op jit(solution)/shard_map/pallas_call | solution.py:180
  54.8 0.5 collective-permute-start.11
  55.3 0.2 select_reduce_fusion.2
  55.5 0.1 collective-permute-start.2
  55.6 0.1 add_reduce_fusion
  55.8 0.5 collective-permute-start.5
  56.3 1.1 %collective-permute-done.11.refs_1_ = f32[64,3584]{1,0:T(8,128)S(1)} collective-permute-done((f32[64,3584]{1,0:T(8,128)S(1)}, f32[64,3584]{1,0:T(8,128)S(1)}, u32[]{:S(2)}, u32[]{:S(2)}) %collective-permute-start.11) | collective-permute-done | bytes 917536 | tf_op jit(solution)/shard_map/ppermute | solution.py:290
  57.4 4.0 %shard_map.80 = (bf16[64,2048]{1,0:T(8,128)(2,1)S(1)}, bf16[64,2048]{1,0:T(8,128)(2,1)S(1)}) custom-call(s32[448]{0:T(512)S(1)} %broadcast_add_fusion.2.rows, s32[225]{0:T(256)S(1)} %minimum_select_fusion.2.columns, f32[64,3584]{1,0:T(8,128)S(1)} %shard_map.79.refs_0_, f32[64,3584]{1,0:T(8,128)S(1)} %collective-permute-done.11.refs_1_, ...), custom_call_target="tpu_custom_call" | custom-call | flops 939524096 | bytes 14680064 | tf_op jit(solution)/shard_map/pallas_call | solution.py:230
  61.4 1.0 collective-permute-start.12
  62.4 1.1 collective-permute-start.13
  63.5 0.0 collective-permute-done.8.refs_1_
  63.5 4.8 %shard_map.78 = f32[128,4096]{1,0:T(8,128)S(1)} custom-call(s32[448]{0:T(512)S(1)} %broadcast_add_fusion.2.rows, s32[225]{0:T(256)S(1)} %minimum_select_fusion.2.columns, f32[128,3584]{1,0:T(8,128)S(1)} %shard_map.77.refs_0_, f32[128,3584]{1,0:T(8,128)S(1)} %collective-permute-done.8.refs_1_, bf16[1792,4096]{1,0:T(8,128)(2,1)} %refs_2_.3), custom_call_target="tpu_custom_call" | custom-call | flops 1879048192 | bytes 14680064 | tf_op jit(solution)/shard_map/pallas_call | solution.py:230
  68.2 0.1 convert.13
  68.4 1.1 collective-permute-done.12
  69.5 2.6 %collective-permute-done.13 = bf16[64,2048]{1,0:T(8,128)(2,1)S(1)} collective-permute-done((bf16[64,2048]{1,0:T(8,128)(2,1)S(1)}, bf16[64,2048]{1,0:T(8,128)(2,1)S(1)}, u32[]{:S(2)}, u32[]{:S(2)}) %collective-permute-start.13) | collective-permute-done | bytes 262176 | tf_op jit(solution)/shard_map/ppermute | solution.py:260
  72.1 0.1 fusion.6
  72.3 1.8 %collective-permute-start.14 = (bf16[64,4096]{1,0:T(8,128)(2,1)S(1)}, bf16[64,4096]{1,0:T(8,128)(2,1)S(1)}, u32[]{:S(2)}, u32[]{:S(2)}) collective-permute-start(bf16[64,4096]{1,0:T(8,128)(2,1)S(1)} %pad_maximum_fusion), channel_id=1, source_target_pairs={{0,4},{4,8},{8,12},{12,14},{14,10},{10,6},{6,2},{2,0},{1,5},{5,9},... | collective-permute-start | bytes 1572872 | tf_op jit(solution)/shard_map/ppermute | solution.py:260
  74.1 0.3 collective-permute-start.15
  74.4 0.0 collective-permute-done.5.refs_3_
  74.4 8.4 %shard_map.76 = f32[320,4096]{1,0:T(8,128)S(1)} custom-call(s32[448]{0:T(512)S(1)} %broadcast_add_fusion.2.rows, s32[225]{0:T(256)S(1)} %minimum_select_fusion.2.columns, f32[192,3584]{1,0:T(8,128)S(1)} %shard_map.74.refs_0_, f32[192,3584]{1,0:T(8,128)S(1)} %collective-permute-done.2.refs_1_, f32[128,3584]{1,0:T(8,128)S(1)} %shard_map.75.refs_2_, ...), custom_call_target="tpu_custom_call" | custom-call | flops 4697620480 | bytes 14680064 | tf_op jit(solution)/shard_map/pallas_call | solution.py:230
  82.8 3.4 %collective-permute-done.14 = bf16[64,4096]{1,0:T(8,128)(2,1)S(1)} collective-permute-done((bf16[64,4096]{1,0:T(8,128)(2,1)S(1)}, bf16[64,4096]{1,0:T(8,128)(2,1)S(1)}, u32[]{:S(2)}, u32[]{:S(2)}) %collective-permute-start.14) | collective-permute-done | bytes 524320 | tf_op jit(solution)/shard_map/ppermute | solution.py:260
  86.2 1.3 %collective-permute-done.15 = bf16[64,4096]{1,0:T(8,128)(2,1)S(1)} collective-permute-done((bf16[64,4096]{1,0:T(8,128)(2,1)S(1)}, bf16[64,4096]{1,0:T(8,128)(2,1)S(1)}, u32[]{:S(2)}, u32[]{:S(2)}) %collective-permute-start.15) | collective-permute-done | bytes 524320 | tf_op jit(solution)/shard_map/ppermute | solution.py:260
  87.5 0.3 fusion.1
  87.8 0.5 collective-permute-start.16
  88.3 1.5 %collective-permute-start.17 = (bf16[64,4096]{1,0:T(8,128)(2,1)S(1)}, bf16[64,4096]{1,0:T(8,128)(2,1)S(1)}, u32[]{:S(2)}, u32[]{:S(2)}) collective-permute-start(bf16[64,4096]{1,0:T(8,128)(2,1)S(1)} %get-tuple-element.30), channel_id=1, source_target_pairs={{4,0},{8,4},{12,8},{14,12},{10,14},{6,10},{2,6},{0,2},{5,1},{9,5},... | collective-permute-start | bytes 1572872 | tf_op jit(solution)/shard_map/ppermute | solution.py:260
  89.9 10.4 %collective-permute-done.16 = bf16[64,4096]{1,0:T(8,128)(2,1)S(1)} collective-permute-done((bf16[64,4096]{1,0:T(8,128)(2,1)S(1)}, bf16[64,4096]{1,0:T(8,128)(2,1)S(1)}, u32[]{:S(2)}, u32[]{:S(2)}) %collective-permute-start.16) | collective-permute-done | bytes 524320 | tf_op jit(solution)/shard_map/ppermute | solution.py:260
  100.3 0.3 collective-permute-done.17
  100.6 0.2 fusion
  100.9 0.5 collective-permute-start.18
  101.3 1.6 %collective-permute-start.19 = (bf16[64,4096]{1,0:T(8,128)(2,1)S(1)}, bf16[64,4096]{1,0:T(8,128)(2,1)S(1)}, u32[]{:S(2)}, u32[]{:S(2)}) collective-permute-start(bf16[64,4096]{1,0:T(8,128)(2,1)S(1)} %get-tuple-element.32), channel_id=1, source_target_pairs={{4,0},{8,4},{12,8},{14,12},{10,14},{6,10},{2,6},{0,2},{5,1},{9,5},... | collective-permute-start | bytes 1572872 | tf_op jit(solution)/shard_map/ppermute | solution.py:260
  102.9 9.4 %collective-permute-done.18 = bf16[64,4096]{1,0:T(8,128)(2,1)S(1)} collective-permute-done((bf16[64,4096]{1,0:T(8,128)(2,1)S(1)}, bf16[64,4096]{1,0:T(8,128)(2,1)S(1)}, u32[]{:S(2)}, u32[]{:S(2)}) %collective-permute-start.18) | collective-permute-done | bytes 524320 | tf_op jit(solution)/shard_map/ppermute | solution.py:260
  112.3 0.3 collective-permute-done.19
  112.6 1.0 fusion.5
  (29 shorter events, 0.3 us)
Async XLA Ops:
  0.0 15.1 %collective-permute-start = (bf16[64,4096]{1,0:T(8,128)(2,1)}, bf16[64,4096]{1,0:T(8,128)(2,1)S(1)}, u32[]{:S(2)}, u32[]{:S(2)}) collective-permute-start(bf16[64,4096]{1,0:T(8,128)(2,1)} %refs_4_.4), channel_id=1, source_target_pairs={{0,4},{4,8},{8,12},{12,14},{14,10},{10,6},{6,2},{2,0},{1,5},{5,9},... | collective-permute-start | bytes 1572872 | tf_op jit(solution)/shard_map/ppermute | solution.py:303
  3.0 13.9 %collective-permute-start.1 = (bf16[64,4096]{1,0:T(8,128)(2,1)}, bf16[64,4096]{1,0:T(8,128)(2,1)S(1)}, u32[]{:S(2)}, u32[]{:S(2)}) collective-permute-start(bf16[64,4096]{1,0:T(8,128)(2,1)} %refs_4_.4), channel_id=1, source_target_pairs={{4,0},{8,4},{12,8},{14,12},{10,14},{6,10},{2,6},{0,2},{5,1},{9,5},... | collective-permute-start | bytes 1572872 | tf_op jit(solution)/shard_map/ppermute | solution.py:303
  6.9 10.2 %copy-start = (bf16[64,4096]{1,0:T(8,128)(2,1)S(1)}, bf16[64,4096]{1,0:T(8,128)(2,1)}, u32[]{:S(2)}) copy-start(bf16[64,4096]{1,0:T(8,128)(2,1)} %refs_4_.4) | copy-start | bytes 1572868
  15.1 13.1 %collective-permute-start.3 = (bf16[64,4096]{1,0:T(8,128)(2,1)S(1)}, bf16[64,4096]{1,0:T(8,128)(2,1)S(1)}, u32[]{:S(2)}, u32[]{:S(2)}) collective-permute-start(bf16[64,4096]{1,0:T(8,128)(2,1)S(1)} %collective-permute-done.refs_5_), channel_id=1, source_target_pairs={{0,4},{4,8},{8,12},{12,14},{14,10},{10,6},{6,2},{2,0},{1,5},{5,9},... | collective-permute-start | bytes 1572872 | tf_op jit(solution)/shard_map/ppermute | solution.py:303
  16.9 12.5 %collective-permute-start.4 = (bf16[64,4096]{1,0:T(8,128)(2,1)S(1)}, bf16[64,4096]{1,0:T(8,128)(2,1)S(1)}, u32[]{:S(2)}, u32[]{:S(2)}) collective-permute-start(bf16[64,4096]{1,0:T(8,128)(2,1)S(1)} %collective-permute-done.1.refs_6_), channel_id=1, source_target_pairs={{4,0},{8,4},{12,8},{14,12},{10,14},{6,10},{2,6},{0,2},{5,1},{9,5},... | collective-permute-start | bytes 1572872 | tf_op jit(solution)/shard_map/ppermute | solution.py:303
  29.4 11.6 %collective-permute-start.6 = (bf16[64,4096]{1,0:T(8,128)(2,1)S(1)}, bf16[64,4096]{1,0:T(8,128)(2,1)S(1)}, u32[]{:S(2)}, u32[]{:S(2)}) collective-permute-start(bf16[64,4096]{1,0:T(8,128)(2,1)S(1)} %collective-permute-done.3.refs_4_), channel_id=1, source_target_pairs={{0,4},{4,8},{8,12},{12,14},{14,10},{10,6},{6,2},{2,0},{1,5},{5,9},... | collective-permute-start | bytes 1572872 | tf_op jit(solution)/shard_map/ppermute | solution.py:303
  31.0 12.0 %collective-permute-start.7 = (bf16[64,4096]{1,0:T(8,128)(2,1)S(1)}, bf16[64,4096]{1,0:T(8,128)(2,1)S(1)}, u32[]{:S(2)}, u32[]{:S(2)}) collective-permute-start(bf16[64,4096]{1,0:T(8,128)(2,1)S(1)} %collective-permute-done.4.refs_5_), channel_id=1, source_target_pairs={{4,0},{8,4},{12,8},{14,12},{10,14},{6,10},{2,6},{0,2},{5,1},{9,5},... | collective-permute-start | bytes 1572872 | tf_op jit(solution)/shard_map/ppermute | solution.py:303
  43.0 7.6 %collective-permute-start.10 = (bf16[64,2048]{1,0:T(8,128)(2,1)S(1)}, bf16[64,2048]{1,0:T(8,128)(2,1)S(1)}, u32[]{:S(2)}, u32[]{:S(2)}) collective-permute-start(bf16[64,2048]{1,0:T(8,128)(2,1)S(1)} %slice.46), channel_id=1, source_target_pairs={{4,0},{8,4},{12,8},{14,12},{10,14},{6,10},{2,6},{0,2},{5,1},{9,5},... | collective-permute-start | bytes 786440 | tf_op jit(solution)/shard_map/ppermute | solution.py:303
  43.6 7.1 %collective-permute-start.9 = (bf16[64,2048]{1,0:T(8,128)(2,1)S(1)}, bf16[64,2048]{1,0:T(8,128)(2,1)S(1)}, u32[]{:S(2)}, u32[]{:S(2)}) collective-permute-start(bf16[64,2048]{1,0:T(8,128)(2,1)S(1)} %slice.45), channel_id=1, source_target_pairs={{0,4},{4,8},{8,12},{12,14},{14,10},{10,6},{6,2},{2,0},{1,5},{5,9},... | collective-permute-start | bytes 786440 | tf_op jit(solution)/shard_map/ppermute | solution.py:303
  50.4 13.1 %collective-permute-start.8 = (f32[128,3584]{1,0:T(8,128)S(1)}, f32[128,3584]{1,0:T(8,128)S(1)}, u32[]{:S(2)}, u32[]{:S(2)}) collective-permute-start(f32[128,3584]{1,0:T(8,128)S(1)} %shard_map.77.refs_0_), channel_id=1, source_target_pairs={{0,1},{1,0},{2,3},{3,2},{4,5},{5,4},{6,7},{7,6},{8,9},{9,8},{10,11... | collective-permute-start | bytes 5505032 | tf_op jit(solution)/shard_map/ppermute | solution.py:290
  54.8 2.6 %collective-permute-start.11 = (f32[64,3584]{1,0:T(8,128)S(1)}, f32[64,3584]{1,0:T(8,128)S(1)}, u32[]{:S(2)}, u32[]{:S(2)}) collective-permute-start(f32[64,3584]{1,0:T(8,128)S(1)} %shard_map.79.refs_0_), channel_id=1, source_target_pairs={{0,1},{1,0},{2,3},{3,2},{4,5},{5,4},{6,7},{7,6},{8,9},{9,8},{10,11... | collective-permute-start | bytes 2752520 | tf_op jit(solution)/shard_map/ppermute | solution.py:290
  55.5 18.9 %collective-permute-start.2 = (f32[192,3584]{1,0:T(8,128)S(1)}, f32[192,3584]{1,0:T(8,128)S(1)}, u32[]{:S(2)}, u32[]{:S(2)}) collective-permute-start(f32[192,3584]{1,0:T(8,128)S(1)} %shard_map.74.refs_0_), channel_id=1, source_target_pairs={{0,1},{1,0},{2,3},{3,2},{4,5},{5,4},{6,7},{7,6},{8,9},{9,8},{10,11... | collective-permute-start | bytes 8257544 | tf_op jit(solution)/shard_map/ppermute | solution.py:290
  55.8 18.7 %collective-permute-start.5 = (f32[128,3584]{1,0:T(8,128)S(1)}, f32[128,3584]{1,0:T(8,128)S(1)}, u32[]{:S(2)}, u32[]{:S(2)}) collective-permute-start(f32[128,3584]{1,0:T(8,128)S(1)} %shard_map.75.refs_2_), channel_id=1, source_target_pairs={{0,1},{1,0},{2,3},{3,2},{4,5},{5,4},{6,7},{7,6},{8,9},{9,8},{10,11... | collective-permute-start | bytes 5505032 | tf_op jit(solution)/shard_map/ppermute | solution.py:290
  61.4 8.1 %collective-permute-start.12 = (bf16[64,2048]{1,0:T(8,128)(2,1)S(1)}, bf16[64,2048]{1,0:T(8,128)(2,1)S(1)}, u32[]{:S(2)}, u32[]{:S(2)}) collective-permute-start(bf16[64,2048]{1,0:T(8,128)(2,1)S(1)} %get-tuple-element.25), channel_id=1, source_target_pairs={{0,4},{4,8},{8,12},{12,14},{14,10},{10,6},{6,2},{2,0},{1,5},{5,9},... | collective-permute-start | bytes 786440 | tf_op jit(solution)/shard_map/ppermute | solution.py:260
  62.4 9.7 %collective-permute-start.13 = (bf16[64,2048]{1,0:T(8,128)(2,1)S(1)}, bf16[64,2048]{1,0:T(8,128)(2,1)S(1)}, u32[]{:S(2)}, u32[]{:S(2)}) collective-permute-start(bf16[64,2048]{1,0:T(8,128)(2,1)S(1)} %get-tuple-element.26), channel_id=1, source_target_pairs={{4,0},{8,4},{12,8},{14,12},{10,14},{6,10},{2,6},{0,2},{5,1},{9,5},... | collective-permute-start | bytes 786440 | tf_op jit(solution)/shard_map/ppermute | solution.py:260
  72.3 13.9 %collective-permute-start.14 = (bf16[64,4096]{1,0:T(8,128)(2,1)S(1)}, bf16[64,4096]{1,0:T(8,128)(2,1)S(1)}, u32[]{:S(2)}, u32[]{:S(2)}) collective-permute-start(bf16[64,4096]{1,0:T(8,128)(2,1)S(1)} %pad_maximum_fusion), channel_id=1, source_target_pairs={{0,4},{4,8},{8,12},{12,14},{14,10},{10,6},{6,2},{2,0},{1,5},{5,9},... | collective-permute-start | bytes 1572872 | tf_op jit(solution)/shard_map/ppermute | solution.py:260
  74.1 13.4 %collective-permute-start.15 = (bf16[64,4096]{1,0:T(8,128)(2,1)S(1)}, bf16[64,4096]{1,0:T(8,128)(2,1)S(1)}, u32[]{:S(2)}, u32[]{:S(2)}) collective-permute-start(bf16[64,4096]{1,0:T(8,128)(2,1)S(1)} %pad_maximum_fusion.1), channel_id=1, source_target_pairs={{4,0},{8,4},{12,8},{14,12},{10,14},{6,10},{2,6},{0,2},{5,1},{9,5},... | collective-permute-start | bytes 1572872 | tf_op jit(solution)/shard_map/ppermute | solution.py:260
  87.8 12.5 %collective-permute-start.16 = (bf16[64,4096]{1,0:T(8,128)(2,1)S(1)}, bf16[64,4096]{1,0:T(8,128)(2,1)S(1)}, u32[]{:S(2)}, u32[]{:S(2)}) collective-permute-start(bf16[64,4096]{1,0:T(8,128)(2,1)S(1)} %get-tuple-element.29), channel_id=1, source_target_pairs={{0,4},{4,8},{8,12},{12,14},{14,10},{10,6},{6,2},{2,0},{1,5},{5,9},... | collective-permute-start | bytes 1572872 | tf_op jit(solution)/shard_map/ppermute | solution.py:260
  88.3 12.3 %collective-permute-start.17 = (bf16[64,4096]{1,0:T(8,128)(2,1)S(1)}, bf16[64,4096]{1,0:T(8,128)(2,1)S(1)}, u32[]{:S(2)}, u32[]{:S(2)}) collective-permute-start(bf16[64,4096]{1,0:T(8,128)(2,1)S(1)} %get-tuple-element.30), channel_id=1, source_target_pairs={{4,0},{8,4},{12,8},{14,12},{10,14},{6,10},{2,6},{0,2},{5,1},{9,5},... | collective-permute-start | bytes 1572872 | tf_op jit(solution)/shard_map/ppermute | solution.py:260
  100.9 11.4 %collective-permute-start.18 = (bf16[64,4096]{1,0:T(8,128)(2,1)S(1)}, bf16[64,4096]{1,0:T(8,128)(2,1)S(1)}, u32[]{:S(2)}, u32[]{:S(2)}) collective-permute-start(bf16[64,4096]{1,0:T(8,128)(2,1)S(1)} %get-tuple-element.31), channel_id=1, source_target_pairs={{0,4},{4,8},{8,12},{12,14},{14,10},{10,6},{6,2},{2,0},{1,5},{5,9},... | collective-permute-start | bytes 1572872 | tf_op jit(solution)/shard_map/ppermute | solution.py:260
  101.3 11.2 %collective-permute-start.19 = (bf16[64,4096]{1,0:T(8,128)(2,1)S(1)}, bf16[64,4096]{1,0:T(8,128)(2,1)S(1)}, u32[]{:S(2)}, u32[]{:S(2)}) collective-permute-start(bf16[64,4096]{1,0:T(8,128)(2,1)S(1)} %get-tuple-element.32), channel_id=1, source_target_pairs={{4,0},{8,4},{12,8},{14,12},{10,14},{6,10},{2,6},{0,2},{5,1},{9,5},... | collective-permute-start | bytes 1572872 | tf_op jit(solution)/shard_map/ppermute | solution.py:260
where the time goes:
time: 114 us
  waiting for transfers between devices  46.3 us (41%)
  Pallas kernels  42.2 us (37%)
  starting transfers between devices  18.7 us (16%)
  other arithmetic  6.04 us (5%)
    ppermute x4, waiting for transfers between devices, scatter(): lax.ppermute(on, 'row', onward).astype(F32)  24.3 us
    pallas_call x4, Pallas kernels, tokens_product(): pl.pallas_call(functools.partial(tokens_kernel, places), out_shape=jax.Sh...  21 us
    pallas_call x3, Pallas kernels, down_product(): pl.pallas_call(functools.partial(down_kernel, groups, opposite), out_shap...  17.1 us
    ppermute x4, waiting for transfers between devices, body(): lax.ppermute(behind, 'row', onward)  13.1 us
    ppermute x4, starting transfers between devices, body(): lax.ppermute(behind, 'row', onward)  8.03 us
    ppermute x4, starting transfers between devices, scatter(): lax.ppermute(ba, 'row', back).astype(F32)  4.51 us
    ppermute x4, waiting for transfers between devices, scatter(): lax.ppermute(ba, 'row', back).astype(F32)  4.5 us
    pallas_call x1, Pallas kernels, pack(): pl.pallas_call(pack_kernel, out_shape=[jax.ShapeDtypeStruct((items[0].sha...  4.01 us
  transfers between devices with their start and end apart: 20, of which 14 were waited for; matrix products, arithmetic and copies ran while one was open for 4% of the time, Pallas kernels for 37%

commit v1 on v0

--- a/solution.py
+++ b/solution.py
@@ -252,21 +252,34 @@
     return lax.optimization_barrier((values, before))[0]
 
 
-def scatter(parts, onward, back, n):
+STREAMS = 2
+
+
+def scatter(opposite, late, onward, back, n):
     far = n // 2
-    on, ba = parts[far]
-    half = on.shape[1]
-    for k in range(far, 0, -1):
-        on, ba = lax.ppermute(on, "row", onward).astype(F32), lax.ppermute(ba, "row", back).astype(F32)
-        if k == 1:
-            return (parts[0][0] + on + ba).astype(BF16)
-        behind, ahead = parts[k - 1]
-        if k == far:
-            on = jnp.concatenate((ahead[:, :half] + on, ahead[:, half:]), axis=1)
-            ba = jnp.concatenate((behind[:, :half], behind[:, half:] + ba), axis=1)
-        else:
-            on, ba = ahead + on, behind + ba
-        on, ba = tie((on.astype(BF16), ba.astype(BF16)))
+    few = opposite[0].shape[0] // STREAMS
+    half = opposite[0].shape[1]
+    cut = [slice(s * few, (s + 1) * few) for s in range(STREAMS)]
+    sent = [[block[rows] for block in opposite] for rows in cut]
+    last = None
+    for k in range(far - 1, -1, -1):
+        blocks = late(k, last)
+        for s, rows in enumerate(cut):
+            on, ba = (lax.ppermute(block, "row", way) for block, way in zip(sent[s], (onward, back)))
+            if last is not None:
+                on, ba = tie((on, ba), last)
+            on, ba = on.astype(F32), ba.astype(F32)
+            if k == 0:
+                last = sent[s] = ((blocks[0][rows] + on + ba).astype(BF16),)
+                continue
+            behind, ahead = (block[rows] for block in blocks)
+            if k == far - 1:
+                on = jnp.concatenate((ahead[:, :half] + on, ahead[:, half:]), axis=1)
+                ba = jnp.concatenate((behind[:, :half], behind[:, half:] + ba), axis=1)
+            else:
+                on, ba = ahead + on, behind + ba
+            last = sent[s] = tie((on.astype(BF16), ba.astype(BF16)))
+    return jnp.concatenate([block for (block,) in sent], axis=0)
 
 
 def body(n, tokens, gate, up, down, gate_mask, up_mask, down_mask):
@@ -303,15 +316,18 @@
         behind, ahead = lax.ppermute(behind, "row", onward), lax.ppermute(ahead, "row", back)
         steps.append((behind, ahead))
     sums += [product((far - 1,)), product((far,))]
-    parts = [None] * (far + 1)
-    parts[far] = down_product(down_items, sums[-1:], down, True)
-    late = down_product(down_items, sums[-2:-1], down, False)
-    early = down_product(down_items, sums[:-2], down, False)
-    parts[0] = (early[:rows],)
-    for k in range(1, far):
-        source, at = (late, 0) if k == far - 1 else (early, (2 * k - 1) * rows)
-        parts[k] = (source[at : at + rows], source[at + rows : at + 2 * rows])
-    return scatter(parts, onward, back, n)
+    near = {}
+
+    def late(k, sent):
+        if k not in near:
+            group = sums[max(k - 1, 0)]
+            parts = down_product(down_items, [group if sent is None else tie(group, sent)], down, False)
+            for i, block in enumerate(((0,), (1, 2)) if k < 2 else ((0, 1),)):
+                near[i if k < 2 else k] = [parts[j * rows : (j + 1) * rows] for j in block]
+        return near[k]
+
+    opposite = tie(sums[-1], *(other for _, other in sums[:-2]))
+    return scatter(down_product(down_items, [opposite], down, True), late, onward, back, n)
 
 
 def solution(mesh):

time: 114 us -> 110 us (0.965)
  waiting for transfers between devices: 46.3 us -> 31.6 us
  starting transfers between devices: 18.7 us -> 28 us
  Pallas kernels: 42.2 us -> 44.4 us
    ppermute x8 -> x16, waiting for transfers between devices: 28.8 us -> 14.7 us  [scatter(): lax.ppermute(block, 'row', way)]
    ppermute x8 -> x16, starting transfers between devices: 8.31 us -> 18.1 us  [scatter(): lax.ppermute(block, 'row', way)]
    ppermute x4, waiting for transfers between devices: 13.1 us -> 11.9 us  [body(): lax.ppermute(behind, 'row', onward)]
    pallas_call x4, Pallas kernels: 21 us -> 22.3 us  [tokens_product(): pl.pallas_call(functools.partial(tokens_kernel, places), out_shape=jax.Sh...]
    pallas_call x3 -> x4, Pallas kernels: 17.1 us -> 18 us  [down_product(): pl.pallas_call(functools.partial(down_kernel, groups, opposite), out_shap...]
  transfers between devices with their start and end apart: 20 -> 28, of which waited for: 14 -> 16; matrix products, arithmetic and copies ran while one was open for 4% -> 5% of each run, Pallas kernels for 37% -> 40%
where the time goes in v1:
time: 110 us; the launch traced here: 111 us
  Pallas kernels  44.4 us (40%)
  waiting for transfers between devices  31.6 us (29%)
  starting transfers between devices  28 us (25%)
  other arithmetic  5.99 us (5%)
    pallas_call x4, Pallas kernels, tokens_product(): pl.pallas_call(functools.partial(tokens_kernel, places), out_shape=jax.Sh...  22.3 us
    ppermute x16, starting transfers between devices, scatter(): lax.ppermute(block, 'row', way)  18.1 us
    pallas_call x4, Pallas kernels, down_product(): pl.pallas_call(functools.partial(down_kernel, groups, opposite), out_shap...  18 us
    ppermute x16, waiting for transfers between devices, scatter(): lax.ppermute(block, 'row', way)  14.7 us
    ppermute x4, waiting for transfers between devices, body(): lax.ppermute(behind, 'row', onward)  11.9 us
    ppermute x4, starting transfers between devices, body(): lax.ppermute(behind, 'row', onward)  7.98 us
    pallas_call x1, Pallas kernels, pack(): pl.pallas_call(pack_kernel, out_shape=[jax.ShapeDtypeStruct((items[0].sha...  4.17 us
    ppermute x4, waiting for transfers between devices, body(): lax.ppermute(ahead, 'row', back)  3.18 us
  transfers between devices with their start and end apart: 28, of which 16 were waited for; matrix products, arithmetic and copies ran while one was open for 5% of the time, Pallas kernels for 40%

profile of v1, /device:TPU:0, one launch (start us, length us, event | category | flops | bytes accessed | tf_op | source)
XLA Modules:
  0.0 110.5 jit_solution(5104525220664246808)
XLA Ops:
  0.0 3.0 %collective-permute-start = (bf16[64,4096]{1,0:T(8,128)(2,1)}, bf16[64,4096]{1,0:T(8,128)(2,1)S(1)}, u32[]{:S(2)}, u32[]{:S(2)}) collective-permute-start(bf16[64,4096]{1,0:T(8,128)(2,1)} %refs_4_.3), channel_id=1, source_target_pairs={{0,4},{4,8},{8,12},{12,14},{14,10},{10,6},{6,2},{2,0},{1,5},{5,9},... | collective-permute-start | bytes 1572872 | tf_op jit(solution)/shard_map/ppermute | solution.py:316
  3.1 0.8 convert_reduce_fusion.4
  3.9 0.1 select_reduce_fusion.8
  4.0 0.8 convert_reduce_fusion.3
  4.9 0.1 select_reduce_fusion.7
  5.0 0.7 convert_reduce_fusion.5
  5.7 0.1 select_reduce_fusion.6
  5.8 0.1 convert_reduce_fusion.1
  6.1 0.5 select_reduce_fusion.3
  6.7 0.3 select_reduce_fusion
  7.0 4.2 %shard_map.73 = (bf16[57344,128]{1,0:T(8,128)(2,1)S(1)}, bf16[57344,128]{1,0:T(8,128)(2,1)S(1)}) custom-call(s32[448]{0:T(512)S(1)} %broadcast_add_fusion.1.refs_0_, s32[225]{0:T(256)S(1)} %get-tuple-element.124.refs_1_, s32[448]{0:T(512)S(1)} %broadcast_add_fusion.refs_2_, s32[225]{0:T(256)S(1)} %get-tuple-element.123.refs_3_, bf16[4096,1792]{1,0:T(8,128)(2,1)} %refs_4_.2, ...), custom_call_target="tpu_custom_call" | custom-call | bytes 14680064 | tf_op jit(solution)/shard_map/pallas_call | solution.py:139
  11.2 0.1 select_reduce_fusion.5
  11.4 3.7 %collective-permute-done.refs_5_ = bf16[64,4096]{1,0:T(8,128)(2,1)S(1)} collective-permute-done((bf16[64,4096]{1,0:T(8,128)(2,1)}, bf16[64,4096]{1,0:T(8,128)(2,1)S(1)}, u32[]{:S(2)}, u32[]{:S(2)}) %collective-permute-start) | collective-permute-done | bytes 524320 | tf_op jit(solution)/shard_map/ppermute | solution.py:316
  15.1 1.8 %collective-permute-start.3 = (bf16[64,4096]{1,0:T(8,128)(2,1)S(1)}, bf16[64,4096]{1,0:T(8,128)(2,1)S(1)}, u32[]{:S(2)}, u32[]{:S(2)}) collective-permute-start(bf16[64,4096]{1,0:T(8,128)(2,1)S(1)} %collective-permute-done.refs_5_), channel_id=1, source_target_pairs={{0,4},{4,8},{8,12},{12,14},{14,10},{10,6},{6,2},{2,0},{1,5},{5,9},... | collective-permute-start | bytes 1572872 | tf_op jit(solution)/shard_map/ppermute | solution.py:316
  16.9 0.2 collective-permute-start.4
  17.1 6.8 %shard_map.74.refs_0_ = f32[192,3584]{1,0:T(8,128)S(1)} custom-call(s32[448]{0:T(512)S(1)} %broadcast_add_fusion.1.refs_0_, s32[225]{0:T(256)S(1)} %get-tuple-element.124.refs_1_, s32[448]{0:T(512)S(1)} %broadcast_add_fusion.refs_2_, s32[225]{0:T(256)S(1)} %get-tuple-element.123.refs_3_, bf16[64,4096]{1,0:T(8,128)(2,1)S(1)} %copy-done, ...), custom_call_target="tpu_custom_call" | custom-call | flops 22548578304 | bytes 117440512 | tf_op jit(solution)/shard_map/pallas_call | solution.py:180
  24.1 4.2 %collective-permute-done.3.refs_4_ = bf16[64,4096]{1,0:T(8,128)(2,1)S(1)} collective-permute-done((bf16[64,4096]{1,0:T(8,128)(2,1)S(1)}, bf16[64,4096]{1,0:T(8,128)(2,1)S(1)}, u32[]{:S(2)}, u32[]{:S(2)}) %collective-permute-start.3) | collective-permute-done | bytes 524320 | tf_op jit(solution)/shard_map/ppermute | solution.py:316
  28.2 1.2 %collective-permute-done.4.refs_5_ = bf16[64,4096]{1,0:T(8,128)(2,1)S(1)} collective-permute-done((bf16[64,4096]{1,0:T(8,128)(2,1)S(1)}, bf16[64,4096]{1,0:T(8,128)(2,1)S(1)}, u32[]{:S(2)}, u32[]{:S(2)}) %collective-permute-start.4) | collective-permute-done | bytes 524320 | tf_op jit(solution)/shard_map/ppermute | solution.py:316
  29.4 1.6 %collective-permute-start.6 = (bf16[64,4096]{1,0:T(8,128)(2,1)S(1)}, bf16[64,4096]{1,0:T(8,128)(2,1)S(1)}, u32[]{:S(2)}, u32[]{:S(2)}) collective-permute-start(bf16[64,4096]{1,0:T(8,128)(2,1)S(1)} %collective-permute-done.3.refs_4_), channel_id=1, source_target_pairs={{0,4},{4,8},{8,12},{12,14},{14,10},{10,6},{6,2},{2,0},{1,5},{5,9},... | collective-permute-start | bytes 1572872 | tf_op jit(solution)/shard_map/ppermute | solution.py:316
  31.0 0.4 collective-permute-start.7
  31.4 5.5 %shard_map.75.refs_0_ = f32[128,3584]{1,0:T(8,128)S(1)} custom-call(s32[448]{0:T(512)S(1)} %broadcast_add_fusion.1.refs_0_, s32[225]{0:T(256)S(1)} %get-tuple-element.124.refs_1_, s32[448]{0:T(512)S(1)} %broadcast_add_fusion.refs_2_, s32[225]{0:T(256)S(1)} %get-tuple-element.123.refs_3_, bf16[64,4096]{1,0:T(8,128)(2,1)S(1)} %collective-permute-done.3.refs_4_, ...), custom_call_target="tpu_custom_call" | custom-call | flops 15032385536 | bytes 117440512 | tf_op jit(solution)/shard_map/pallas_call | solution.py:180
  37.0 4.0 %collective-permute-done.6.refs_4_ = bf16[64,4096]{1,0:T(8,128)(2,1)S(1)} collective-permute-done((bf16[64,4096]{1,0:T(8,128)(2,1)S(1)}, bf16[64,4096]{1,0:T(8,128)(2,1)S(1)}, u32[]{:S(2)}, u32[]{:S(2)}) %collective-permute-start.6) | collective-permute-done | bytes 524320 | tf_op jit(solution)/shard_map/ppermute | solution.py:316
  41.0 2.0 %collective-permute-done.7.refs_5_ = bf16[64,4096]{1,0:T(8,128)(2,1)S(1)} collective-permute-done((bf16[64,4096]{1,0:T(8,128)(2,1)S(1)}, bf16[64,4096]{1,0:T(8,128)(2,1)S(1)}, u32[]{:S(2)}, u32[]{:S(2)}) %collective-permute-start.7) | collective-permute-done | bytes 524320 | tf_op jit(solution)/shard_map/ppermute | solution.py:316
  43.0 0.5 collective-permute-start.10
  43.5 1.6 %collective-permute-start.9 = (bf16[64,2048]{1,0:T(8,128)(2,1)S(1)}, bf16[64,2048]{1,0:T(8,128)(2,1)S(1)}, u32[]{:S(2)}, u32[]{:S(2)}) collective-permute-start(bf16[64,2048]{1,0:T(8,128)(2,1)S(1)} %slice.110), channel_id=1, source_target_pairs={{0,4},{4,8},{8,12},{12,14},{14,10},{10,6},{6,2},{2,0},{1,5},{5,9},... | collective-permute-start | bytes 786440 | tf_op jit(solution)/shard_map/ppermute | solution.py:316
  45.1 5.5 %shard_map.76.refs_0_ = f32[128,3584]{1,0:T(8,128)S(1)} custom-call(s32[448]{0:T(512)S(1)} %broadcast_add_fusion.1.refs_0_, s32[225]{0:T(256)S(1)} %get-tuple-element.124.refs_1_, s32[448]{0:T(512)S(1)} %broadcast_add_fusion.refs_2_, s32[225]{0:T(256)S(1)} %get-tuple-element.123.refs_3_, bf16[64,4096]{1,0:T(8,128)(2,1)S(1)} %collective-permute-done.6.refs_4_, ...), custom_call_target="tpu_custom_call" | custom-call | flops 15032385536 | bytes 117440512 | tf_op jit(solution)/shard_map/pallas_call | solution.py:180
  50.7 4.4 %shard_map.78.refs_0_ = f32[64,3584]{1,0:T(8,128)S(1)} custom-call(s32[448]{0:T(512)S(1)} %broadcast_add_fusion.1.refs_0_, s32[225]{0:T(256)S(1)} %get-tuple-element.124.refs_1_, s32[448]{0:T(512)S(1)} %broadcast_add_fusion.refs_2_, s32[225]{0:T(256)S(1)} %get-tuple-element.123.refs_3_, bf16[64,2048]{1,0:T(8,128)(2,1)S(1)} %collective-permute-done.9.refs_4_, ...), custom_call_target="tpu_custom_call" | custom-call | flops 7516192768 | bytes 117440512 | tf_op jit(solution)/shard_map/pallas_call | solution.py:180
  55.1 0.5 collective-permute-start.11
  55.7 0.2 select_reduce_fusion.2
  55.9 1.9 %collective-permute-done.11.refs_1_ = f32[64,3584]{1,0:T(8,128)S(1)} collective-permute-done((f32[64,3584]{1,0:T(8,128)S(1)}, f32[64,3584]{1,0:T(8,128)S(1)}, u32[]{:S(2)}, u32[]{:S(2)}) %collective-permute-start.11) | collective-permute-done | bytes 917536 | tf_op jit(solution)/shard_map/ppermute | solution.py:303
  57.8 3.7 %shard_map.79 = (bf16[64,2048]{1,0:T(8,128)(2,1)S(1)}, bf16[64,2048]{1,0:T(8,128)(2,1)S(1)}) custom-call(s32[448]{0:T(512)S(1)} %broadcast_add_fusion.2.rows, s32[225]{0:T(256)S(1)} %minimum_select_fusion.2.columns, f32[64,3584]{1,0:T(8,128)S(1)} %shard_map.78.refs_0_, f32[64,3584]{1,0:T(8,128)S(1)} %collective-permute-done.11.refs_1_, ...), custom_call_target="tpu_custom_call" | custom-call | flops 939524096 | bytes 14680064 | tf_op jit(solution)/shard_map/pallas_call | solution.py:230
  61.5 3.3 %collective-permute-start.14 = (bf16[32,2048]{1,0:T(8,128)(2,1)S(1)}, bf16[32,2048]{1,0:T(8,128)(2,1)S(1)}, u32[]{:S(2)}, u32[]{:S(2)}) collective-permute-start(bf16[32,2048]{1,0:T(8,128)(2,1)S(1)} %get-tuple-element.119), channel_id=1, source_target_pairs={{0,4},{4,8},{8,12},{12,14},{14,10},{10,6},{6,2},{2,0},{1,5},{5,9},... | collective-permute-start | bytes 393224 | tf_op jit(solution)/shard_map/ppermute | solution.py:268
  64.8 1.7 %collective-permute-start.12 = (bf16[32,2048]{1,0:T(8,128)(2,1)S(1)}, bf16[32,2048]{1,0:T(8,128)(2,1)S(1)}, u32[]{:S(2)}, u32[]{:S(2)}) collective-permute-start(bf16[32,2048]{1,0:T(8,128)(2,1)S(1)} %get-tuple-element.120), channel_id=1, source_target_pairs={{0,4},{4,8},{8,12},{12,14},{14,10},{10,6},{6,2},{2,0},{1,5},{5,9},... | collective-permute-start | bytes 393224 | tf_op jit(solution)/shard_map/ppermute | solution.py:268
  66.5 0.4 collective-permute-start.15
  66.9 4.4 %shard_map.77 = f32[128,4096]{1,0:T(8,128)S(1)} custom-call(s32[448]{0:T(512)S(1)} %broadcast_add_fusion.2.rows, s32[225]{0:T(256)S(1)} %minimum_select_fusion.2.columns, f32[128,3584]{1,0:T(8,128)S(1)} %shard_map.76.refs_0_, f32[128,3584]{1,0:T(8,128)S(1)} %collective-permute-done.8.refs_1_, bf16[1792,4096]{1,0:T(8,128)(2,1)} %refs_2_.7), custom_call_target="tpu_custom_call" | custom-call | flops 1879048192 | bytes 14680064 | tf_op jit(solution)/shard_map/pallas_call | solution.py:230
  71.3 0.1 convert.23
  71.5 1.4 %collective-permute-done.15 = bf16[32,2048]{1,0:T(8,128)(2,1)S(1)} collective-permute-done((bf16[32,2048]{1,0:T(8,128)(2,1)S(1)}, bf16[32,2048]{1,0:T(8,128)(2,1)S(1)}, u32[]{:S(2)}, u32[]{:S(2)}) %collective-permute-start.15) | collective-permute-done | bytes 131104 | tf_op jit(solution)/shard_map/ppermute | solution.py:268
  73.0 1.3 %collective-permute-start.18 = (bf16[32,4096]{1,0:T(8,128)(2,1)S(1)}, bf16[32,4096]{1,0:T(8,128)(2,1)S(1)}, u32[]{:S(2)}, u32[]{:S(2)}) collective-permute-start(bf16[32,4096]{1,0:T(8,128)(2,1)S(1)} %pad_maximum_fusion.1), channel_id=1, source_target_pairs={{0,4},{4,8},{8,12},{12,14},{14,10},{10,6},{6,2},{2,0},{1,5},{5,9},... | collective-permute-start | bytes 786440 | tf_op jit(solution)/shard_map/ppermute | solution.py:268
  74.3 0.8 collective-permute-start.19
  75.2 1.3 %collective-permute-start.16 = (bf16[32,4096]{1,0:T(8,128)(2,1)S(1)}, bf16[32,4096]{1,0:T(8,128)(2,1)S(1)}, u32[]{:S(2)}, u32[]{:S(2)}) collective-permute-start(bf16[32,4096]{1,0:T(8,128)(2,1)S(1)} %pad_maximum_fusion.3), channel_id=1, source_target_pairs={{0,4},{4,8},{8,12},{12,14},{14,10},{10,6},{6,2},{2,0},{1,5},{5,9},... | collective-permute-start | bytes 786440 | tf_op jit(solution)/shard_map/ppermute | solution.py:268
  76.5 0.8 collective-permute-start.17
  77.3 4.4 %shard_map.80 = f32[128,4096]{1,0:T(8,128)S(1)} custom-call(s32[448]{0:T(512)S(1)} %broadcast_add_fusion.2.rows, s32[225]{0:T(256)S(1)} %minimum_select_fusion.2.columns, f32[128,3584]{1,0:T(8,128)S(1)} %shard_map.75.refs_0_, f32[128,3584]{1,0:T(8,128)S(1)} %collective-permute-done.5.refs_1_, bf16[1792,4096]{1,0:T(8,128)(2,1)} %refs_2_.7), custom_call_target="tpu_custom_call" | custom-call | flops 1879048192 | bytes 14680064 | tf_op jit(solution)/shard_map/pallas_call | solution.py:230
  81.7 0.5 collective-permute-done.18
  82.3 1.3 %collective-permute-done.19 = bf16[32,4096]{1,0:T(8,128)(2,1)S(1)} collective-permute-done((bf16[32,4096]{1,0:T(8,128)(2,1)S(1)}, bf16[32,4096]{1,0:T(8,128)(2,1)S(1)}, u32[]{:S(2)}, u32[]{:S(2)}) %collective-permute-start.19) | collective-permute-done | bytes 262176 | tf_op jit(solution)/shard_map/ppermute | solution.py:268
  83.6 0.1 fusion.9
  83.7 1.4 %collective-permute-start.20 = (bf16[32,4096]{1,0:T(8,128)(2,1)S(1)}, bf16[32,4096]{1,0:T(8,128)(2,1)S(1)}, u32[]{:S(2)}, u32[]{:S(2)}) collective-permute-start(bf16[32,4096]{1,0:T(8,128)(2,1)S(1)} %get-tuple-element.65), channel_id=1, source_target_pairs={{0,4},{4,8},{8,12},{12,14},{14,10},{10,6},{6,2},{2,0},{1,5},{5,9},... | collective-permute-start | bytes 786440 | tf_op jit(solution)/shard_map/ppermute | solution.py:268
  85.1 0.6 collective-permute-start.21
  85.8 2.0 %collective-permute-done.16 = bf16[32,4096]{1,0:T(8,128)(2,1)S(1)} collective-permute-done((bf16[32,4096]{1,0:T(8,128)(2,1)S(1)}, bf16[32,4096]{1,0:T(8,128)(2,1)S(1)}, u32[]{:S(2)}, u32[]{:S(2)}) %collective-permute-start.16) | collective-permute-done | bytes 262176 | tf_op jit(solution)/shard_map/ppermute | solution.py:268
  87.8 1.4 %collective-permute-done.17 = bf16[32,4096]{1,0:T(8,128)(2,1)S(1)} collective-permute-done((bf16[32,4096]{1,0:T(8,128)(2,1)S(1)}, bf16[32,4096]{1,0:T(8,128)(2,1)S(1)}, u32[]{:S(2)}, u32[]{:S(2)}) %collective-permute-start.17) | collective-permute-done | bytes 262176 | tf_op jit(solution)/shard_map/ppermute | solution.py:268
  89.2 0.1 fusion.8
  89.3 1.4 %collective-permute-start.24 = (bf16[32,4096]{1,0:T(8,128)(2,1)S(1)}, bf16[32,4096]{1,0:T(8,128)(2,1)S(1)}, u32[]{:S(2)}, u32[]{:S(2)}) collective-permute-start(bf16[32,4096]{1,0:T(8,128)(2,1)S(1)} %get-tuple-element.69), channel_id=1, source_target_pairs={{0,4},{4,8},{8,12},{12,14},{14,10},{10,6},{6,2},{2,0},{1,5},{5,9},... | collective-permute-start | bytes 786440 | tf_op jit(solution)/shard_map/ppermute | solution.py:268
  90.7 0.6 collective-permute-start.25
  91.4 5.5 %shard_map.81 = f32[192,4096]{1,0:T(8,128)S(1)} custom-call(s32[448]{0:T(512)S(1)} %broadcast_add_fusion.2.rows, s32[225]{0:T(256)S(1)} %minimum_select_fusion.2.columns, f32[192,3584]{1,0:T(8,128)S(1)} %shard_map.74.refs_0_, f32[192,3584]{1,0:T(8,128)S(1)} %collective-permute-done.2.refs_1_, bf16[1792,4096]{1,0:T(8,128)(2,1)} %refs_2_.7), custom_call_target="tpu_custom_call" | custom-call | flops 2818572288 | bytes 14680064 | tf_op jit(solution)/shard_map/pallas_call | solution.py:230
  97.0 2.3 %collective-permute-start.22 = (bf16[32,4096]{1,0:T(8,128)(2,1)S(1)}, bf16[32,4096]{1,0:T(8,128)(2,1)S(1)}, u32[]{:S(2)}, u32[]{:S(2)}) collective-permute-start(bf16[32,4096]{1,0:T(8,128)(2,1)S(1)} %get-tuple-element.75), channel_id=1, source_target_pairs={{0,4},{4,8},{8,12},{12,14},{14,10},{10,6},{6,2},{2,0},{1,5},{5,9},... | collective-permute-start | bytes 786440 | tf_op jit(solution)/shard_map/ppermute | solution.py:268
  99.3 0.8 collective-permute-done.25
  100.2 1.8 %collective-permute-start.26 = (bf16[32,4096]{1,0:T(8,128)(2,1)S(1)}, bf16[32,4096]{1,0:T(8,128)(2,1)S(1)}, u32[]{:S(2)}, u32[]{:S(2)}) collective-permute-start(bf16[32,4096]{1,0:T(8,128)(2,1)S(1)} %get-tuple-element.79), channel_id=1, source_target_pairs={{0,4},{4,8},{8,12},{12,14},{14,10},{10,6},{6,2},{2,0},{1,5},{5,9},... | collective-permute-start | bytes 786440 | tf_op jit(solution)/shard_map/ppermute | solution.py:268
  102.0 0.3 collective-permute-start.27
  102.2 2.5 %collective-permute-done.22 = bf16[32,4096]{1,0:T(8,128)(2,1)S(1)} collective-permute-done((bf16[32,4096]{1,0:T(8,128)(2,1)S(1)}, bf16[32,4096]{1,0:T(8,128)(2,1)S(1)}, u32[]{:S(2)}, u32[]{:S(2)}) %collective-permute-start.22) | collective-permute-done | bytes 262176 | tf_op jit(solution)/shard_map/ppermute | solution.py:268
  104.7 2.0 %collective-permute-done.23 = bf16[32,4096]{1,0:T(8,128)(2,1)S(1)} collective-permute-done((bf16[32,4096]{1,0:T(8,128)(2,1)S(1)}, bf16[32,4096]{1,0:T(8,128)(2,1)S(1)}, u32[]{:S(2)}, u32[]{:S(2)}) %collective-permute-start.23) | collective-permute-done | bytes 262176 | tf_op jit(solution)/shard_map/ppermute | solution.py:268
  106.8 0.1 fusion.7
  106.9 0.7 collective-permute-done.26
  107.5 2.0 %collective-permute-done.27 = bf16[32,4096]{1,0:T(8,128)(2,1)S(1)} collective-permute-done((bf16[32,4096]{1,0:T(8,128)(2,1)S(1)}, bf16[32,4096]{1,0:T(8,128)(2,1)S(1)}, u32[]{:S(2)}, u32[]{:S(2)}) %collective-permute-start.27) | collective-permute-done | bytes 262176 | tf_op jit(solution)/shard_map/ppermute | solution.py:268
  109.6 0.1 fusion.1
  109.7 0.8 pad_maximum_fusion
  (55 shorter events, 1.1 us)
Async XLA Ops:
  0.0 15.1 %collective-permute-start = (bf16[64,4096]{1,0:T(8,128)(2,1)}, bf16[64,4096]{1,0:T(8,128)(2,1)S(1)}, u32[]{:S(2)}, u32[]{:S(2)}) collective-permute-start(bf16[64,4096]{1,0:T(8,128)(2,1)} %refs_4_.3), channel_id=1, source_target_pairs={{0,4},{4,8},{8,12},{12,14},{14,10},{10,6},{6,2},{2,0},{1,5},{5,9},... | collective-permute-start | bytes 1572872 | tf_op jit(solution)/shard_map/ppermute | solution.py:316
  3.0 13.9 %collective-permute-start.1 = (bf16[64,4096]{1,0:T(8,128)(2,1)}, bf16[64,4096]{1,0:T(8,128)(2,1)S(1)}, u32[]{:S(2)}, u32[]{:S(2)}) collective-permute-start(bf16[64,4096]{1,0:T(8,128)(2,1)} %refs_4_.3), channel_id=1, source_target_pairs={{4,0},{8,4},{12,8},{14,12},{10,14},{6,10},{2,6},{0,2},{5,1},{9,5},... | collective-permute-start | bytes 1572872 | tf_op jit(solution)/shard_map/ppermute | solution.py:316
  7.0 10.1 %copy-start = (bf16[64,4096]{1,0:T(8,128)(2,1)S(1)}, bf16[64,4096]{1,0:T(8,128)(2,1)}, u32[]{:S(2)}) copy-start(bf16[64,4096]{1,0:T(8,128)(2,1)} %refs_4_.3) | copy-start | bytes 1572868
  15.1 13.1 %collective-permute-start.3 = (bf16[64,4096]{1,0:T(8,128)(2,1)S(1)}, bf16[64,4096]{1,0:T(8,128)(2,1)S(1)}, u32[]{:S(2)}, u32[]{:S(2)}) collective-permute-start(bf16[64,4096]{1,0:T(8,128)(2,1)S(1)} %collective-permute-done.refs_5_), channel_id=1, source_target_pairs={{0,4},{4,8},{8,12},{12,14},{14,10},{10,6},{6,2},{2,0},{1,5},{5,9},... | collective-permute-start | bytes 1572872 | tf_op jit(solution)/shard_map/ppermute | solution.py:316
  16.9 12.5 %collective-permute-start.4 = (bf16[64,4096]{1,0:T(8,128)(2,1)S(1)}, bf16[64,4096]{1,0:T(8,128)(2,1)S(1)}, u32[]{:S(2)}, u32[]{:S(2)}) collective-permute-start(bf16[64,4096]{1,0:T(8,128)(2,1)S(1)} %collective-permute-done.1.refs_6_), channel_id=1, source_target_pairs={{4,0},{8,4},{12,8},{14,12},{10,14},{6,10},{2,6},{0,2},{5,1},{9,5},... | collective-permute-start | bytes 1572872 | tf_op jit(solution)/shard_map/ppermute | solution.py:316
  24.0 33.8 %collective-permute-start.2 = (f32[192,3584]{1,0:T(8,128)S(1)}, f32[192,3584]{1,0:T(8,128)S(1)}, u32[]{:S(2)}, u32[]{:S(2)}) collective-permute-start(f32[192,3584]{1,0:T(8,128)S(1)} %shard_map.74.refs_0_), channel_id=1, source_target_pairs={{0,1},{1,0},{2,3},{3,2},{4,5},{5,4},{6,7},{7,6},{8,9},{9,8},{10,11... | collective-permute-start | bytes 8257544 | tf_op jit(solution)/shard_map/ppermute | solution.py:303
  29.4 11.6 %collective-permute-start.6 = (bf16[64,4096]{1,0:T(8,128)(2,1)S(1)}, bf16[64,4096]{1,0:T(8,128)(2,1)S(1)}, u32[]{:S(2)}, u32[]{:S(2)}) collective-permute-start(bf16[64,4096]{1,0:T(8,128)(2,1)S(1)} %collective-permute-done.3.refs_4_), channel_id=1, source_target_pairs={{0,4},{4,8},{8,12},{12,14},{14,10},{10,6},{6,2},{2,0},{1,5},{5,9},... | collective-permute-start | bytes 1572872 | tf_op jit(solution)/shard_map/ppermute | solution.py:316
  31.0 12.0 %collective-permute-start.7 = (bf16[64,4096]{1,0:T(8,128)(2,1)S(1)}, bf16[64,4096]{1,0:T(8,128)(2,1)S(1)}, u32[]{:S(2)}, u32[]{:S(2)}) collective-permute-start(bf16[64,4096]{1,0:T(8,128)(2,1)S(1)} %collective-permute-done.4.refs_5_), channel_id=1, source_target_pairs={{4,0},{8,4},{12,8},{14,12},{10,14},{6,10},{2,6},{0,2},{5,1},{9,5},... | collective-permute-start | bytes 1572872 | tf_op jit(solution)/shard_map/ppermute | solution.py:316
  37.0 20.8 %collective-permute-start.5 = (f32[128,3584]{1,0:T(8,128)S(1)}, f32[128,3584]{1,0:T(8,128)S(1)}, u32[]{:S(2)}, u32[]{:S(2)}) collective-permute-start(f32[128,3584]{1,0:T(8,128)S(1)} %shard_map.75.refs_0_), channel_id=1, source_target_pairs={{0,1},{1,0},{2,3},{3,2},{4,5},{5,4},{6,7},{7,6},{8,9},{9,8},{10,11... | collective-permute-start | bytes 5505032 | tf_op jit(solution)/shard_map/ppermute | solution.py:303
  43.0 7.7 %collective-permute-start.10 = (bf16[64,2048]{1,0:T(8,128)(2,1)S(1)}, bf16[64,2048]{1,0:T(8,128)(2,1)S(1)}, u32[]{:S(2)}, u32[]{:S(2)}) collective-permute-start(bf16[64,2048]{1,0:T(8,128)(2,1)S(1)} %slice.111), channel_id=1, source_target_pairs={{4,0},{8,4},{12,8},{14,12},{10,14},{6,10},{2,6},{0,2},{5,1},{9,5},... | collective-permute-start | bytes 786440 | tf_op jit(solution)/shard_map/ppermute | solution.py:316
  43.5 7.2 %collective-permute-start.9 = (bf16[64,2048]{1,0:T(8,128)(2,1)S(1)}, bf16[64,2048]{1,0:T(8,128)(2,1)S(1)}, u32[]{:S(2)}, u32[]{:S(2)}) collective-permute-start(bf16[64,2048]{1,0:T(8,128)(2,1)S(1)} %slice.110), channel_id=1, source_target_pairs={{0,4},{4,8},{8,12},{12,14},{14,10},{10,6},{6,2},{2,0},{1,5},{5,9},... | collective-permute-start | bytes 786440 | tf_op jit(solution)/shard_map/ppermute | solution.py:316
  50.6 16.3 %collective-permute-start.8 = (f32[128,3584]{1,0:T(8,128)S(1)}, f32[128,3584]{1,0:T(8,128)S(1)}, u32[]{:S(2)}, u32[]{:S(2)}) collective-permute-start(f32[128,3584]{1,0:T(8,128)S(1)} %shard_map.76.refs_0_), channel_id=1, source_target_pairs={{0,1},{1,0},{2,3},{3,2},{4,5},{5,4},{6,7},{7,6},{8,9},{9,8},{10,11... | collective-permute-start | bytes 5505032 | tf_op jit(solution)/shard_map/ppermute | solution.py:303
  55.1 2.6 %collective-permute-start.11 = (f32[64,3584]{1,0:T(8,128)S(1)}, f32[64,3584]{1,0:T(8,128)S(1)}, u32[]{:S(2)}, u32[]{:S(2)}) collective-permute-start(f32[64,3584]{1,0:T(8,128)S(1)} %shard_map.78.refs_0_), channel_id=1, source_target_pairs={{0,1},{1,0},{2,3},{3,2},{4,5},{5,4},{6,7},{7,6},{8,9},{9,8},{10,11... | collective-permute-start | bytes 2752520 | tf_op jit(solution)/shard_map/ppermute | solution.py:303
  61.5 10.0 %collective-permute-start.14 = (bf16[32,2048]{1,0:T(8,128)(2,1)S(1)}, bf16[32,2048]{1,0:T(8,128)(2,1)S(1)}, u32[]{:S(2)}, u32[]{:S(2)}) collective-permute-start(bf16[32,2048]{1,0:T(8,128)(2,1)S(1)} %get-tuple-element.119), channel_id=1, source_target_pairs={{0,4},{4,8},{8,12},{12,14},{14,10},{10,6},{6,2},{2,0},{1,5},{5,9},... | collective-permute-start | bytes 393224 | tf_op jit(solution)/shard_map/ppermute | solution.py:268
  64.8 10.4 %collective-permute-start.12 = (bf16[32,2048]{1,0:T(8,128)(2,1)S(1)}, bf16[32,2048]{1,0:T(8,128)(2,1)S(1)}, u32[]{:S(2)}, u32[]{:S(2)}) collective-permute-start(bf16[32,2048]{1,0:T(8,128)(2,1)S(1)} %get-tuple-element.120), channel_id=1, source_target_pairs={{0,4},{4,8},{8,12},{12,14},{14,10},{10,6},{6,2},{2,0},{1,5},{5,9},... | collective-permute-start | bytes 393224 | tf_op jit(solution)/shard_map/ppermute | solution.py:268
  66.5 6.5 %collective-permute-start.15 = (bf16[32,2048]{1,0:T(8,128)(2,1)S(1)}, bf16[32,2048]{1,0:T(8,128)(2,1)S(1)}, u32[]{:S(2)}, u32[]{:S(2)}) collective-permute-start(bf16[32,2048]{1,0:T(8,128)(2,1)S(1)} %get-tuple-element.117), channel_id=1, source_target_pairs={{4,0},{8,4},{12,8},{14,12},{10,14},{6,10},{2,6},{0,2},{5,1},{9,5},... | collective-permute-start | bytes 393224 | tf_op jit(solution)/shard_map/ppermute | solution.py:268
  66.9 8.3 %collective-permute-start.13 = (bf16[32,2048]{1,0:T(8,128)(2,1)S(1)}, bf16[32,2048]{1,0:T(8,128)(2,1)S(1)}, u32[]{:S(2)}, u32[]{:S(2)}) collective-permute-start(bf16[32,2048]{1,0:T(8,128)(2,1)S(1)} %get-tuple-element.118), channel_id=1, source_target_pairs={{4,0},{8,4},{12,8},{14,12},{10,14},{6,10},{2,6},{0,2},{5,1},{9,5},... | collective-permute-start | bytes 393224 | tf_op jit(solution)/shard_map/ppermute | solution.py:268
  73.0 9.2 %collective-permute-start.18 = (bf16[32,4096]{1,0:T(8,128)(2,1)S(1)}, bf16[32,4096]{1,0:T(8,128)(2,1)S(1)}, u32[]{:S(2)}, u32[]{:S(2)}) collective-permute-start(bf16[32,4096]{1,0:T(8,128)(2,1)S(1)} %pad_maximum_fusion.1), channel_id=1, source_target_pairs={{0,4},{4,8},{8,12},{12,14},{14,10},{10,6},{6,2},{2,0},{1,5},{5,9},... | collective-permute-start | bytes 786440 | tf_op jit(solution)/shard_map/ppermute | solution.py:268
  74.3 9.2 %collective-permute-start.19 = (bf16[32,4096]{1,0:T(8,128)(2,1)S(1)}, bf16[32,4096]{1,0:T(8,128)(2,1)S(1)}, u32[]{:S(2)}, u32[]{:S(2)}) collective-permute-start(bf16[32,4096]{1,0:T(8,128)(2,1)S(1)} %pad_maximum_fusion.2), channel_id=1, source_target_pairs={{4,0},{8,4},{12,8},{14,12},{10,14},{6,10},{2,6},{0,2},{5,1},{9,5},... | collective-permute-start | bytes 786440 | tf_op jit(solution)/shard_map/ppermute | solution.py:268
  75.2 12.5 %collective-permute-start.16 = (bf16[32,4096]{1,0:T(8,128)(2,1)S(1)}, bf16[32,4096]{1,0:T(8,128)(2,1)S(1)}, u32[]{:S(2)}, u32[]{:S(2)}) collective-permute-start(bf16[32,4096]{1,0:T(8,128)(2,1)S(1)} %pad_maximum_fusion.3), channel_id=1, source_target_pairs={{0,4},{4,8},{8,12},{12,14},{14,10},{10,6},{6,2},{2,0},{1,5},{5,9},... | collective-permute-start | bytes 786440 | tf_op jit(solution)/shard_map/ppermute | solution.py:268
  76.5 12.7 %collective-permute-start.17 = (bf16[32,4096]{1,0:T(8,128)(2,1)S(1)}, bf16[32,4096]{1,0:T(8,128)(2,1)S(1)}, u32[]{:S(2)}, u32[]{:S(2)}) collective-permute-start(bf16[32,4096]{1,0:T(8,128)(2,1)S(1)} %pad_maximum_fusion.4), channel_id=1, source_target_pairs={{4,0},{8,4},{12,8},{14,12},{10,14},{6,10},{2,6},{0,2},{5,1},{9,5},... | collective-permute-start | bytes 786440 | tf_op jit(solution)/shard_map/ppermute | solution.py:268
  83.7 13.2 %collective-permute-start.20 = (bf16[32,4096]{1,0:T(8,128)(2,1)S(1)}, bf16[32,4096]{1,0:T(8,128)(2,1)S(1)}, u32[]{:S(2)}, u32[]{:S(2)}) collective-permute-start(bf16[32,4096]{1,0:T(8,128)(2,1)S(1)} %get-tuple-element.65), channel_id=1, source_target_pairs={{0,4},{4,8},{8,12},{12,14},{14,10},{10,6},{6,2},{2,0},{1,5},{5,9},... | collective-permute-start | bytes 786440 | tf_op jit(solution)/shard_map/ppermute | solution.py:268
  85.1 11.8 %collective-permute-start.21 = (bf16[32,4096]{1,0:T(8,128)(2,1)S(1)}, bf16[32,4096]{1,0:T(8,128)(2,1)S(1)}, u32[]{:S(2)}, u32[]{:S(2)}) collective-permute-start(bf16[32,4096]{1,0:T(8,128)(2,1)S(1)} %get-tuple-element.66), channel_id=1, source_target_pairs={{4,0},{8,4},{12,8},{14,12},{10,14},{6,10},{2,6},{0,2},{5,1},{9,5},... | collective-permute-start | bytes 786440 | tf_op jit(solution)/shard_map/ppermute | solution.py:268
  89.3 10.0 %collective-permute-start.24 = (bf16[32,4096]{1,0:T(8,128)(2,1)S(1)}, bf16[32,4096]{1,0:T(8,128)(2,1)S(1)}, u32[]{:S(2)}, u32[]{:S(2)}) collective-permute-start(bf16[32,4096]{1,0:T(8,128)(2,1)S(1)} %get-tuple-element.69), channel_id=1, source_target_pairs={{0,4},{4,8},{8,12},{12,14},{14,10},{10,6},{6,2},{2,0},{1,5},{5,9},... | collective-permute-start | bytes 786440 | tf_op jit(solution)/shard_map/ppermute | solution.py:268
  90.7 9.3 %collective-permute-start.25 = (bf16[32,4096]{1,0:T(8,128)(2,1)S(1)}, bf16[32,4096]{1,0:T(8,128)(2,1)S(1)}, u32[]{:S(2)}, u32[]{:S(2)}) collective-permute-start(bf16[32,4096]{1,0:T(8,128)(2,1)S(1)} %get-tuple-element.70), channel_id=1, source_target_pairs={{4,0},{8,4},{12,8},{14,12},{10,14},{6,10},{2,6},{0,2},{5,1},{9,5},... | collective-permute-start | bytes 786440 | tf_op jit(solution)/shard_map/ppermute | solution.py:268
  97.0 7.7 %collective-permute-start.22 = (bf16[32,4096]{1,0:T(8,128)(2,1)S(1)}, bf16[32,4096]{1,0:T(8,128)(2,1)S(1)}, u32[]{:S(2)}, u32[]{:S(2)}) collective-permute-start(bf16[32,4096]{1,0:T(8,128)(2,1)S(1)} %get-tuple-element.75), channel_id=1, source_target_pairs={{0,4},{4,8},{8,12},{12,14},{14,10},{10,6},{6,2},{2,0},{1,5},{5,9},... | collective-permute-start | bytes 786440 | tf_op jit(solution)/shard_map/ppermute | solution.py:268
  99.3 7.5 %collective-permute-start.23 = (bf16[32,4096]{1,0:T(8,128)(2,1)S(1)}, bf16[32,4096]{1,0:T(8,128)(2,1)S(1)}, u32[]{:S(2)}, u32[]{:S(2)}) collective-permute-start(bf16[32,4096]{1,0:T(8,128)(2,1)S(1)} %get-tuple-element.76), channel_id=1, source_target_pairs={{4,0},{8,4},{12,8},{14,12},{10,14},{6,10},{2,6},{0,2},{5,1},{9,5},... | collective-permute-start | bytes 786440 | tf_op jit(solution)/shard_map/ppermute | solution.py:268
  100.2 7.4 %collective-permute-start.26 = (bf16[32,4096]{1,0:T(8,128)(2,1)S(1)}, bf16[32,4096]{1,0:T(8,128)(2,1)S(1)}, u32[]{:S(2)}, u32[]{:S(2)}) collective-permute-start(bf16[32,4096]{1,0:T(8,128)(2,1)S(1)} %get-tuple-element.79), channel_id=1, source_target_pairs={{0,4},{4,8},{8,12},{12,14},{14,10},{10,6},{6,2},{2,0},{1,5},{5,9},... | collective-permute-start | bytes 786440 | tf_op jit(solution)/shard_map/ppermute | solution.py:268
  102.0 7.6 %collective-permute-start.27 = (bf16[32,4096]{1,0:T(8,128)(2,1)S(1)}, bf16[32,4096]{1,0:T(8,128)(2,1)S(1)}, u32[]{:S(2)}, u32[]{:S(2)}) collective-permute-start(bf16[32,4096]{1,0:T(8,128)(2,1)S(1)} %get-tuple-element.80), channel_id=1, source_target_pairs={{4,0},{8,4},{12,8},{14,12},{10,14},{6,10},{2,6},{0,2},{5,1},{9,5},... | collective-permute-start | bytes 786440 | tf_op jit(solution)/shard_map/ppermute | solution.py:268

commit v2 on v1

v2 whole, which is shorter than its diff:
```python
import functools

import jax
import jax.numpy as jnp
from jax import lax
from jax.experimental import pallas as pl
from jax.experimental.pallas import tpu as pltpu
from jax.sharding import PartitionSpec as P

SIDE = 128
DEPTH = 2
ITEMS = 8
TRIP = ITEMS * DEPTH
HELD = 2
F32 = jnp.float32
BF16 = jnp.bfloat16


def round_up(n, unit):
    return -(-n // unit) * unit


def kept_items(mask):
    deep, wide = mask.shape
    kept = (mask != 0).astype(jnp.int32).T
    row = jnp.arange(deep)
    before = jnp.sum(jnp.where(row[None, :, None] > row[None, None, :], kept[:, None, :], 0), axis=2)
    filled = round_up(jnp.sum(kept, axis=1), DEPTH)
    column = jnp.arange(wide)
    ends = jnp.sum(jnp.where(column[:, None] >= column[None, :], filled[None, :], 0), axis=1)
    place = jnp.where(kept != 0, (ends - filled)[:, None] + before, -1)
    spots = jnp.arange(round_up(wide * round_up(deep, DEPTH), TRIP))
    rows = deep + jnp.sum(
        jnp.where(place[None] == spots[:, None, None], row[None, None, :] - deep, 0), axis=(1, 2)
    )
    items = jnp.arange(spots.shape[0] // DEPTH + 1)
    columns = jnp.sum((ends[None, :] <= items[:, None] * DEPTH).astype(jnp.int32), axis=1)
    trips = round_up(jnp.max(ends[None, :] + items[:, None], axis=1) - items, TRIP) // (TRIP)
    columns = jnp.where(items == items.shape[0] - 1, trips, jnp.minimum(columns, wide - 1))
    return rows.astype(jnp.int32), columns.astype(jnp.int32)


def trips_of(columns):
    return columns[columns.shape[0] - 1]


def block_of(i):
    return pl.ds(pl.multiple_of(i * SIDE, SIDE), SIDE)


def trip_blocks(ref, k):
    return ref.at[pl.ds(pl.multiple_of(k * TRIP * SIDE, TRIP * SIDE), TRIP * SIDE), :]


def start_trip(k, rows, columns, weight, into, sem):
    deep = weight.shape[0] // SIDE
    for t in range(TRIP):
        i = rows[k * TRIP + t]
        pltpu.make_async_copy(
            weight.at[block_of(jnp.where(i == deep, 0, i)), block_of(columns[k * ITEMS + t // DEPTH])],
            into.at[pl.ds(t * SIDE, SIDE), :],
            sem,
        ).start()


def wait_trip(into, sem):
    pltpu.make_async_copy(into, into, sem).wait()


def multiply_trip(k, rows, columns, held, blocks, total):
    deep = DEPTH * SIDE
    for t in range(ITEMS):
        item = k * ITEMS + t
        lhs = jnp.concatenate([held[:, block_of(rows[item * DEPTH + d])] for d in range(DEPTH)], axis=1)
        rhs = blocks[pl.ds(t * deep, deep), :]
        total[:, block_of(columns[item])] += jnp.dot(lhs, rhs, preferred_element_type=F32)


def multiply(rows, columns, packed, weight, held, spill, sem, total):
    def ready(k, _):
        multiply_trip(k, rows, columns, held, trip_blocks(packed, k), total)
        return 0

    def beyond(k, _):
        start_trip(k, rows, columns, weight, spill, sem)
        wait_trip(spill, sem)
        multiply_trip(k, rows, columns, held, spill, total)
        return 0

    trips = trips_of(columns)
    room = packed.shape[0] // (TRIP * SIDE)
    lax.fori_loop(0, jnp.minimum(trips, room), ready, 0)
    lax.fori_loop(room, jnp.maximum(trips, room), beyond, 0)


SPILL = [pltpu.VMEM((TRIP * SIDE, SIDE), BF16), pltpu.SemaphoreType.DMA(())]
SMEM = pl.BlockSpec(memory_space=pltpu.SMEM)
VMEM = pl.BlockSpec(memory_space=pltpu.VMEM)
HBM = pl.BlockSpec(memory_space=pltpu.HBM)


def packed_trips(columns, packed):
    return jnp.minimum(trips_of(columns), packed.shape[0] // (TRIP * SIDE))


def start_packing(rows, columns, weight, packed, sem):
    def start(k, _):
        start_trip(k, rows, columns, weight, trip_blocks(packed, k), sem)
        return 0

    lax.fori_loop(0, packed_trips(columns, packed), start, 0)


def wait_packing(columns, packed, sem):
    def wait(k, _):
        wait_trip(trip_blocks(packed, k), sem)
        return 0

    lax.fori_loop(0, packed_trips(columns, packed), wait, 0)


def packed_shape(items):
    return jax.ShapeDtypeStruct((-(-items[0].shape[0] // (TRIP * HELD)) * TRIP * SIDE, SIDE), BF16)


def pack_kernel(count, *refs):
    lists, weights, packed, sems = refs[: 2 * count], refs[2 * count : 3 * count], refs[3 * count : 4 * count], refs[-1]
    for w in range(count):
        start_packing(*lists[2 * w : 2 * w + 2], weights[w], packed[w], sems.at[w])
    for w in range(count):
        wait_packing(lists[2 * w + 1], packed[w], sems.at[w])


def pack(weights, items):
    count = len(weights)
    return pl.pallas_call(
        functools.partial(pack_kernel, count),
        out_shape=[packed_shape(one) for one in items],
        in_specs=[SMEM] * (2 * count) + [HBM] * count,
        out_specs=[VMEM] * count,
        scratch_shapes=[pltpu.SemaphoreType.DMA((count,))],
        compiler_params=pltpu.CompilerParams(vmem_limit_bytes=1 << 20),
        cost_estimate=pl.CostEstimate(
            flops=0, bytes_accessed=sum(2 * weight.size for weight in weights), transcendentals=0
        ),
    )(*(one for pair in items for one in pair), *weights)


def tokens_kernel(places, packs, *refs):
    lists, refs = refs[:4], refs[4:]
    pieces, refs = refs[: len(places)], refs[len(places) :]
    packed, (gate, up), refs = refs[:2], refs[2:4], refs[4:]
    if packs:
        rows, columns, down, out, down_packed, held, sems, spill, sem, pack_sem = refs
    else:
        out, held, sems, spill, sem = refs
    deep, width = gate.shape
    copies = [
        pltpu.make_async_copy(piece, held.at[pl.ds(row, piece.shape[0]), pl.ds(column, piece.shape[1])], sems.at[k])
        for k, (piece, (row, column)) in enumerate(zip(pieces, places))
    ]
    for copy in copies:
        copy.start()
    if packs:
        start_packing(rows, columns, down, down_packed, pack_sem)
    held[:, deep:] = jnp.zeros((held.shape[0], SIDE), BF16)
    out[...] = jnp.zeros(out.shape, F32)
    for copy in copies:
        copy.wait()
    for w, weight in enumerate((gate, up)):
        total = out.at[:, pl.ds(w * width, width)]
        multiply(*lists[2 * w : 2 * w + 2], packed[w], weight, held, spill, sem, total)
    if packs:
        wait_packing(columns, down_packed, pack_sem)


def tokens_product(items, pieces, places, packed, gate, up, to_pack=()):
    rows = max(row + piece.shape[0] for piece, (row, _) in zip(pieces, places))
    deep, width = gate.shape
    return pl.pallas_call(
        functools.partial(tokens_kernel, places, bool(to_pack)),
        out_shape=[jax.ShapeDtypeStruct((rows, 2 * width), F32)] + ([packed_shape(to_pack)] if to_pack else []),
        in_specs=[SMEM] * 4 + [VMEM] * (len(pieces) + 2) + [HBM] * 2 + ([SMEM, SMEM, HBM] if to_pack else []),
        out_specs=[VMEM] * (2 if to_pack else 1),
        scratch_shapes=[pltpu.VMEM((rows, deep + SIDE), BF16), pltpu.SemaphoreType.DMA((len(pieces),)), *SPILL]
        + ([pltpu.SemaphoreType.DMA(())] if to_pack else []),
        compiler_params=pltpu.CompilerParams(vmem_limit_bytes=6 << 20),
        cost_estimate=pl.CostEstimate(
            flops=16 * rows * deep * width, bytes_accessed=16 * deep * width, transcendentals=0
        ),
    )(*(one for pair in items for one in pair), *pieces, *packed, gate, up, *to_pack)


def down_kernel(groups, opposite, rows, columns, *refs):
    sums, refs = refs[: 2 * groups], refs[2 * groups :]
    if opposite:
        packed, down, on, back, total, held, spill, sem = refs
    else:
        packed, down, total, held, spill, sem = refs
    deep = down.shape[0]
    held[:, deep:] = jnp.zeros((held.shape[0], SIDE), BF16)
    total[...] = jnp.zeros(total.shape, F32)
    at = 0
    for g in range(groups):
        mine, other = sums[2 * g : 2 * g + 2]

        def some(s, _, at=at, mine=mine, other=other):
            here = pl.ds(pl.multiple_of(s * 16, 16), 16)
            value = mine[here, :] + other[here, :]
            silu = value[:, :deep] / (1.0 + jnp.exp(-value[:, :deep]))
            held[pl.ds(pl.multiple_of(at + s * 16, 16), 16), pl.ds(0, deep)] = (silu * value[:, deep:]).astype(BF16)
            return 0

        lax.fori_loop(0, mine.shape[0] // 16, some, 0)
        at += mine.shape[0]
    multiply(rows, columns, packed, down, held, spill, sem, total)
    if opposite:
        half = on.shape[1]
        on[...] = total[:, pl.ds(0, half)].astype(BF16)
        back[...] = total[:, pl.ds(half, half)].astype(BF16)


def down_product(items, sums, packed, down, opposite):
    deep, width = down.shape
    groups = len(sums)
    rows = sum(mine.shape[0] for mine, _ in sums)
    whole = pltpu.VMEM((rows, width), F32)
    half = jax.ShapeDtypeStruct((rows, width // 2), BF16)
    return pl.pallas_call(
        functools.partial(down_kernel, groups, opposite),
        out_shape=(half, half) if opposite else jax.ShapeDtypeStruct((rows, width), F32),
        in_specs=[SMEM] * 2 + [VMEM] * (2 * groups + 1) + [HBM],
        out_specs=(VMEM, VMEM) if opposite else VMEM,
        scratch_shapes=([whole] if opposite else []) + [pltpu.VMEM((rows, deep + SIDE), BF16), *SPILL],
        compiler_params=pltpu.CompilerParams(vmem_limit_bytes=6 << 20),
        cost_estimate=pl.CostEstimate(
            flops=rows * deep * width * 2, bytes_accessed=deep * width * 2, transcendentals=rows * deep
        ),
    )(*items, *(part for pair in sums for part in pair), packed, down)


def ring_of(n):
    order = list(range(n)) if n > 8 else list(range(0, n, 2)) + list(range(n - 1, 0, -2))
    onward = [(order[k], order[(k + 1) % n]) for k in range(n)]
    return onward, [(b, a) for a, b in onward]


def tie(values, *before):
    return lax.optimization_barrier((values, before))[0]


STREAMS = 2


def scatter(opposite, late, onward, back, n):
    far = n // 2
    few = opposite[0].shape[0] // STREAMS
    half = opposite[0].shape[1]
    cut = [slice(s * few, (s + 1) * few) for s in range(STREAMS)]
    sent = [[block[rows] for block in opposite] for rows in cut]
    last = None
    for k in range(far - 1, -1, -1):
        blocks = late(k, last)
        for s, rows in enumerate(cut):
            on, ba = (lax.ppermute(block, "row", way) for block, way in zip(sent[s], (onward, back)))
            if k == 0:
                on, ba = tie((on, ba), last)
                last = sent[s] = ((blocks[0][rows] + on.astype(F32) + ba.astype(F32)).astype(BF16),)
                continue
            both = []
            for side, (sum_, block) in enumerate(((on, blocks[1]), (ba, blocks[0]))):
                sum_ = (sum_ if last is None else tie(sum_, last)).astype(F32)
                block = block[rows]
                if k < far - 1:
                    block = block + sum_
                elif side == 0:
                    block = jnp.concatenate((block[:, :half] + sum_, block[:, half:]), axis=1)
                else:
                    block = jnp.concatenate((block[:, :half], block[:, half:] + sum_), axis=1)
                last = block.astype(BF16)
                both.append(last)
            sent[s] = both
    return jnp.concatenate([block for (block,) in sent], axis=0)


def body(n, tokens, gate, up, down, gate_mask, up_mask, down_mask):
    onward, back = ring_of(n)
    swap = [(0, 1), (1, 0)]
    far = n // 2
    half = tokens.shape[1] // 2
    gate_items, up_items, down_items = kept_items(gate_mask), kept_items(up_mask), kept_items(down_mask)
    rows = tokens.shape[0]
    def product(group, to_pack=()):
        pieces, places = [], []
        at = 0
        for k in group:
            for piece in steps[k]:
                pieces.append(piece)
                places.append((at, 0))
                at += rows
        if group[-1] == far:
            places[-2:] = [(at - 2 * rows, 0), (at - 2 * rows, half)]
        mine, *more = tokens_product((gate_items, up_items), pieces, places, packed, gate, up, to_pack)
        return mine, lax.ppermute(mine, "col", swap), *more

    gate, up, down = (pltpu.with_memory_space_constraint(w, pltpu.HBM) for w in (gate, up, down))
    packed = pack((gate, up), (gate_items, up_items))
    behind = ahead = tokens
    steps = [(tokens,)]
    sums = []
    for k in range(1, far + 1):
        if k == 3:
            *first, down_packed = product((0, 1), (*down_items, down))
            sums.append(tuple(first))
        elif k > 3:
            sums.append(product((k - 2,)))
        if k > 2:
            behind, ahead = tie(behind, sums[-1][0]), tie(ahead, sums[-1][0])
        if k == far:
            behind, ahead = behind[:, :half], ahead[:, half:]
        behind, ahead = lax.ppermute(behind, "row", onward), lax.ppermute(ahead, "row", back)
        steps.append((behind, ahead))
    sums.append(product((far - 1,)))
    steps[far] = tie(steps[far], sums[-1][0])
    sums.append(product((far,)))
    near = {}

    def late(k, sent):
        if k not in near:
            group = sums[max(k - 1, 0)]
            parts = down_product(down_items, [group if sent is None else tie(group, sent)], down_packed, down, False)
            for i, block in enumerate(((0,), (1, 2)) if k < 2 else ((0, 1),)):
                near[i if k < 2 else k] = [parts[j * rows : (j + 1) * rows] for j in block]
        return near[k]

    opposite = tie(sums[-1], *(other for _, other in sums[:-2]))
    return scatter(down_product(down_items, [opposite], down_packed, down, True), late, onward, back, n)


def solution(mesh):
    return jax.shard_map(
        functools.partial(body, mesh.shape["row"]),
        mesh=mesh,
        in_specs=(
            P(("groups", "row"), "col"),
            P("col", "row"),
            P("col", "row"),
            P("row", "col"),
            P("col", "row"),
            P("col", "row"),
            P("row", "col"),
        ),
        out_specs=P(("groups", "row"), "col"),
        check_vma=False,
    )
```

time: 110 us -> 108 us (0.982)
  waiting for transfers between devices: 31.6 us -> 24.4 us
  Pallas kernels: 44.4 us -> 46.7 us
  starting transfers between devices: 28 us -> 29.7 us
    ppermute x4, waiting for transfers between devices: 11.9 us -> 3.04 us  [body(): lax.ppermute(behind, 'row', onward)]
    pallas_call x5, Pallas kernels: 26.4 us -> 30.3 us  [the longest x4 25.7 us: tokens_product(): pl.pallas_call(functools.partial(tokens_kernel, places, bool(to_pack)), o...]
    ppermute x4, waiting for transfers between devices: 3.18 us -> 7.07 us  [body(): lax.ppermute(ahead, 'row', back)]
    ppermute x16, waiting for transfers between devices: 14.7 us -> 12.3 us  [scatter(): lax.ppermute(block, 'row', way)]
    ppermute x16, starting transfers between devices: 18.1 us -> 19.8 us  [scatter(): lax.ppermute(block, 'row', way)]
    pallas_call x4, Pallas kernels: 18 us -> 16.4 us  [down_product(): pl.pallas_call(functools.partial(down_kernel, groups, opposite), out_shap...]
  transfers between devices with their start and end apart: 28 -> 28, of which waited for: 16 -> 9; matrix products, arithmetic and copies ran while one was open for 5% -> 5% of each run, Pallas kernels for 40% -> 43%
where the time goes in v2:
time: 108 us; the launch traced here: 107 us
  Pallas kernels  46.7 us (43%)
  starting transfers between devices  29.7 us (28%)
  waiting for transfers between devices  24.4 us (23%)
  other arithmetic  6.07 us (6%)
    pallas_call x4, Pallas kernels, tokens_product(): pl.pallas_call(functools.partial(tokens_kernel, places, bool(to_pack)), o...  25.7 us
    ppermute x16, starting transfers between devices, scatter(): lax.ppermute(block, 'row', way)  19.8 us
    pallas_call x4, Pallas kernels, down_product(): pl.pallas_call(functools.partial(down_kernel, groups, opposite), out_shap...  16.4 us
    ppermute x16, waiting for transfers between devices, scatter(): lax.ppermute(block, 'row', way)  12.3 us
    ppermute x4, starting transfers between devices, body(): lax.ppermute(behind, 'row', onward)  7.42 us
    ppermute x4, waiting for transfers between devices, body(): lax.ppermute(ahead, 'row', back)  7.07 us
    pallas_call x1, Pallas kernels, pack(): pl.pallas_call(functools.partial(pack_kernel, count), out_shape=[packed_s...  4.65 us
    ppermute x4, waiting for transfers between devices, body(): lax.ppermute(behind, 'row', onward)  3.04 us
  transfers between devices with their start and end apart: 28, of which 9 were waited for; matrix products, arithmetic and copies ran while one was open for 5% of the time, Pallas kernels for 43%

profile of v2, /device:TPU:0, one launch (start us, length us, event | category | flops | bytes accessed | tf_op | source)
XLA Modules:
  0.0 107.4 jit_solution(10572211721370885662)
XLA Ops:
  0.0 3.0 %collective-permute-start = (bf16[64,4096]{1,0:T(8,128)(2,1)}, bf16[64,4096]{1,0:T(8,128)(2,1)S(1)}, u32[]{:S(2)}, u32[]{:S(2)}) collective-permute-start(bf16[64,4096]{1,0:T(8,128)(2,1)} %refs_4_.3), channel_id=1, source_target_pairs={{0,4},{4,8},{8,12},{12,14},{14,10},{10,6},{6,2},{2,0},{1,5},{5,9},... | collective-permute-start | bytes 1572872 | tf_op jit(solution)/shard_map/ppermute | solution.py:321
  3.1 0.8 convert_reduce_fusion.3
  3.9 0.8 convert_reduce_fusion.4
  4.7 0.1 select_reduce_fusion.8
  4.9 0.1 select_reduce_fusion.7
  5.0 0.5 select_reduce_fusion.3
  5.6 0.1 add_select_fusion
  5.6 0.3 select_reduce_fusion
  6.0 0.1 convert_reduce_fusion.1
  6.0 0.7 convert_reduce_fusion.5
  6.8 0.1 select_reduce_fusion.6
  6.9 0.1 select_reduce_fusion.5
  7.1 0.2 select_reduce_fusion.2
  7.3 4.7 %shard_map.73 = (bf16[28672,128]{1,0:T(8,128)(2,1)S(1)}, bf16[28672,128]{1,0:T(8,128)(2,1)S(1)}) custom-call(s32[448]{0:T(512)S(1)} %broadcast_add_fusion.1.refs_0_, s32[225]{0:T(256)S(1)} %get-tuple-element.98.refs_1_, s32[448]{0:T(512)S(1)} %broadcast_add_fusion.refs_2_, s32[225]{0:T(256)S(1)} %get-tuple-element.97.refs_3_, bf16[4096,1792]{1,0:T(8,128)(2,1)} %refs_8_.5, ...), custom_call_target="tpu_custom_call" | custom-call | bytes 29360128 | tf_op jit(solution)/shard_map/pallas_call | solution.py:136
  11.9 0.1 add_reduce_fusion
  12.1 3.0 %collective-permute-done.refs_5_ = bf16[64,4096]{1,0:T(8,128)(2,1)S(1)} collective-permute-done((bf16[64,4096]{1,0:T(8,128)(2,1)}, bf16[64,4096]{1,0:T(8,128)(2,1)S(1)}, u32[]{:S(2)}, u32[]{:S(2)}) %collective-permute-start) | collective-permute-done | bytes 524320 | tf_op jit(solution)/shard_map/ppermute | solution.py:321
  15.1 1.8 %collective-permute-start.3 = (bf16[64,4096]{1,0:T(8,128)(2,1)S(1)}, bf16[64,4096]{1,0:T(8,128)(2,1)S(1)}, u32[]{:S(2)}, u32[]{:S(2)}) collective-permute-start(bf16[64,4096]{1,0:T(8,128)(2,1)S(1)} %collective-permute-done.refs_5_), channel_id=1, source_target_pairs={{0,4},{4,8},{8,12},{12,14},{14,10},{10,6},{6,2},{2,0},{1,5},{5,9},... | collective-permute-start | bytes 1572872 | tf_op jit(solution)/shard_map/ppermute | solution.py:321
  16.9 0.2 collective-permute-start.4
  17.1 8.5 %shard_map.74 = (f32[192,3584]{1,0:T(8,128)S(1)}, bf16[28672,128]{1,0:T(8,128)(2,1)S(1)}) custom-call(s32[448]{0:T(512)S(1)} %broadcast_add_fusion.1.refs_0_, s32[225]{0:T(256)S(1)} %get-tuple-element.98.refs_1_, s32[448]{0:T(512)S(1)} %broadcast_add_fusion.refs_2_, s32[225]{0:T(256)S(1)} %get-tuple-element.97.refs_3_, bf16[64,4096]{1,0:T(8,128)(2,1)S(1)} %copy-done, ...), custom_call_target="tpu_custom_call" | custom-call | flops 22548578304 | bytes 117440512 | tf_op jit(solution)/shard_map/pallas_call | solution.py:180
  25.6 0.1 collective-permute-start.2
  25.7 3.7 %collective-permute-done.4.refs_5_ = bf16[64,4096]{1,0:T(8,128)(2,1)S(1)} collective-permute-done((bf16[64,4096]{1,0:T(8,128)(2,1)S(1)}, bf16[64,4096]{1,0:T(8,128)(2,1)S(1)}, u32[]{:S(2)}, u32[]{:S(2)}) %collective-permute-start.4) | collective-permute-done | bytes 524320 | tf_op jit(solution)/shard_map/ppermute | solution.py:321
  29.4 0.5 collective-permute-start.7
  30.0 1.5 %collective-permute-start.6 = (bf16[64,4096]{1,0:T(8,128)(2,1)S(1)}, bf16[64,4096]{1,0:T(8,128)(2,1)S(1)}, u32[]{:S(2)}, u32[]{:S(2)}) collective-permute-start(bf16[64,4096]{1,0:T(8,128)(2,1)S(1)} %collective-permute-done.3.refs_4_), channel_id=1, source_target_pairs={{0,4},{4,8},{8,12},{12,14},{14,10},{10,6},{6,2},{2,0},{1,5},{5,9},... | collective-permute-start | bytes 1572872 | tf_op jit(solution)/shard_map/ppermute | solution.py:321
  31.4 6.2 %shard_map.75.refs_0_ = f32[128,3584]{1,0:T(8,128)S(1)} custom-call(s32[448]{0:T(512)S(1)} %broadcast_add_fusion.1.refs_0_, s32[225]{0:T(256)S(1)} %get-tuple-element.98.refs_1_, s32[448]{0:T(512)S(1)} %broadcast_add_fusion.refs_2_, s32[225]{0:T(256)S(1)} %get-tuple-element.97.refs_3_, bf16[64,4096]{1,0:T(8,128)(2,1)S(1)} %collective-permute-done.3.refs_4_, ...), custom_call_target="tpu_custom_call" | custom-call | flops 15032385536 | bytes 117440512 | tf_op jit(solution)/shard_map/pallas_call | solution.py:180
  37.6 0.1 collective-permute-start.5
  37.7 3.3 %collective-permute-done.7.refs_5_ = bf16[64,4096]{1,0:T(8,128)(2,1)S(1)} collective-permute-done((bf16[64,4096]{1,0:T(8,128)(2,1)S(1)}, bf16[64,4096]{1,0:T(8,128)(2,1)S(1)}, u32[]{:S(2)}, u32[]{:S(2)}) %collective-permute-start.7) | collective-permute-done | bytes 524320 | tf_op jit(solution)/shard_map/ppermute | solution.py:321
  41.0 1.0 collective-permute-start.10
  42.1 1.1 %collective-permute-start.9 = (bf16[64,2048]{1,0:T(8,128)(2,1)S(1)}, bf16[64,2048]{1,0:T(8,128)(2,1)S(1)}, u32[]{:S(2)}, u32[]{:S(2)}) collective-permute-start(bf16[64,2048]{1,0:T(8,128)(2,1)S(1)} %slice.111), channel_id=1, source_target_pairs={{0,4},{4,8},{8,12},{12,14},{14,10},{10,6},{6,2},{2,0},{1,5},{5,9},... | collective-permute-start | bytes 786440 | tf_op jit(solution)/shard_map/ppermute | solution.py:321
  43.2 6.2 %shard_map.76.refs_0_ = f32[128,3584]{1,0:T(8,128)S(1)} custom-call(s32[448]{0:T(512)S(1)} %broadcast_add_fusion.1.refs_0_, s32[225]{0:T(256)S(1)} %get-tuple-element.98.refs_1_, s32[448]{0:T(512)S(1)} %broadcast_add_fusion.refs_2_, s32[225]{0:T(256)S(1)} %get-tuple-element.97.refs_3_, bf16[64,4096]{1,0:T(8,128)(2,1)S(1)} %collective-permute-done.6.refs_4_, ...), custom_call_target="tpu_custom_call" | custom-call | flops 15032385536 | bytes 117440512 | tf_op jit(solution)/shard_map/pallas_call | solution.py:180
  49.4 4.9 %shard_map.78.refs_0_ = f32[64,3584]{1,0:T(8,128)S(1)} custom-call(s32[448]{0:T(512)S(1)} %broadcast_add_fusion.1.refs_0_, s32[225]{0:T(256)S(1)} %get-tuple-element.98.refs_1_, s32[448]{0:T(512)S(1)} %broadcast_add_fusion.refs_2_, s32[225]{0:T(256)S(1)} %get-tuple-element.97.refs_3_, bf16[64,2048]{1,0:T(8,128)(2,1)S(1)} %collective-permute-done.9.refs_4_, ...), custom_call_target="tpu_custom_call" | custom-call | flops 7516192768 | bytes 117440512 | tf_op jit(solution)/shard_map/pallas_call | solution.py:180
  54.3 0.1 collective-permute-start.11
  54.4 0.5 collective-permute-start.8
  54.9 2.0 %collective-permute-done.11.refs_1_ = f32[64,3584]{1,0:T(8,128)S(1)} collective-permute-done((f32[64,3584]{1,0:T(8,128)S(1)}, f32[64,3584]{1,0:T(8,128)S(1)}, u32[]{:S(2)}, u32[]{:S(2)}) %collective-permute-start.11) | collective-permute-done | bytes 917536 | tf_op jit(solution)/shard_map/ppermute | solution.py:304
  56.8 3.1 %shard_map.79 = (bf16[64,2048]{1,0:T(8,128)(2,1)S(1)}, bf16[64,2048]{1,0:T(8,128)(2,1)S(1)}) custom-call(s32[448]{0:T(512)S(1)} %broadcast_add_fusion.2.refs_11_.rows, s32[225]{0:T(256)S(1)} %minimum_select_fusion.2.refs_12_.columns, f32[64,3584]{1,0:T(8,128)S(1)} %shard_map.78.refs_0_, f32[64,3584]{1,0:T(8,128)S(1)} %collective-permute-done.11.refs_1_, ...), custom_call_target="tpu_custom_call" | custom-call | flops 939524096 | bytes 14680064 | tf_op jit(solution)/shard_map/pallas_call | solution.py:229
  60.0 3.1 %collective-permute-start.15 = (bf16[32,2048]{1,0:T(8,128)(2,1)S(1)}, bf16[32,2048]{1,0:T(8,128)(2,1)S(1)}, u32[]{:S(2)}, u32[]{:S(2)}) collective-permute-start(bf16[32,2048]{1,0:T(8,128)(2,1)S(1)} %get-tuple-element.91), channel_id=1, source_target_pairs={{0,4},{4,8},{8,12},{12,14},{14,10},{10,6},{6,2},{2,0},{1,5},{5,9},... | collective-permute-start | bytes 393224 | tf_op jit(solution)/shard_map/ppermute | solution.py:265
  63.2 2.0 %collective-permute-start.13 = (bf16[32,2048]{1,0:T(8,128)(2,1)S(1)}, bf16[32,2048]{1,0:T(8,128)(2,1)S(1)}, u32[]{:S(2)}, u32[]{:S(2)}) collective-permute-start(bf16[32,2048]{1,0:T(8,128)(2,1)S(1)} %get-tuple-element.92), channel_id=1, source_target_pairs={{0,4},{4,8},{8,12},{12,14},{14,10},{10,6},{6,2},{2,0},{1,5},{5,9},... | collective-permute-start | bytes 393224 | tf_op jit(solution)/shard_map/ppermute | solution.py:265
  65.2 0.1 collective-permute-start.12
  65.2 4.1 %shard_map.77 = f32[128,4096]{1,0:T(8,128)S(1)} custom-call(s32[448]{0:T(512)S(1)} %broadcast_add_fusion.2.refs_11_.rows, s32[225]{0:T(256)S(1)} %minimum_select_fusion.2.refs_12_.columns, f32[128,3584]{1,0:T(8,128)S(1)} %shard_map.76.refs_0_, f32[128,3584]{1,0:T(8,128)S(1)} %collective-permute-done.8.refs_1_, ...), custom_call_target="tpu_custom_call" | custom-call | flops 1879048192 | bytes 14680064 | tf_op jit(solution)/shard_map/pallas_call | solution.py:229
  69.3 0.1 convert.22
  69.6 2.3 %collective-permute-start.19 = (bf16[32,4096]{1,0:T(8,128)(2,1)S(1)}, bf16[32,4096]{1,0:T(8,128)(2,1)S(1)}, u32[]{:S(2)}, u32[]{:S(2)}) collective-permute-start(bf16[32,4096]{1,0:T(8,128)(2,1)S(1)} %pad_maximum_fusion.1), channel_id=1, source_target_pairs={{0,4},{4,8},{8,12},{12,14},{14,10},{10,6},{6,2},{2,0},{1,5},{5,9},... | collective-permute-start | bytes 786440 | tf_op jit(solution)/shard_map/ppermute | solution.py:265
  72.0 0.1 collective-permute-start.18
  72.1 2.1 %collective-permute-start.17 = (bf16[32,4096]{1,0:T(8,128)(2,1)S(1)}, bf16[32,4096]{1,0:T(8,128)(2,1)S(1)}, u32[]{:S(2)}, u32[]{:S(2)}) collective-permute-start(bf16[32,4096]{1,0:T(8,128)(2,1)S(1)} %pad_maximum_fusion.3), channel_id=1, source_target_pairs={{0,4},{4,8},{8,12},{12,14},{14,10},{10,6},{6,2},{2,0},{1,5},{5,9},... | collective-permute-start | bytes 786440 | tf_op jit(solution)/shard_map/ppermute | solution.py:265
  74.2 0.1 collective-permute-start.16
  74.3 4.0 %shard_map.80 = f32[128,4096]{1,0:T(8,128)S(1)} custom-call(s32[448]{0:T(512)S(1)} %broadcast_add_fusion.2.refs_11_.rows, s32[225]{0:T(256)S(1)} %minimum_select_fusion.2.refs_12_.columns, f32[128,3584]{1,0:T(8,128)S(1)} %shard_map.75.refs_0_, f32[128,3584]{1,0:T(8,128)S(1)} %collective-permute-done.5.refs_1_, ...), custom_call_target="tpu_custom_call" | custom-call | flops 1879048192 | bytes 14680064 | tf_op jit(solution)/shard_map/pallas_call | solution.py:229
  78.3 0.5 collective-permute-done.19
  78.9 2.6 %collective-permute-start.20 = (bf16[32,4096]{1,0:T(8,128)(2,1)S(1)}, bf16[32,4096]{1,0:T(8,128)(2,1)S(1)}, u32[]{:S(2)}, u32[]{:S(2)}) collective-permute-start(bf16[32,4096]{1,0:T(8,128)(2,1)S(1)} %fusion.8), channel_id=1, source_target_pairs={{0,4},{4,8},{8,12},{12,14},{14,10},{10,6},{6,2},{2,0},{1,5},{5,9},... | collective-permute-start | bytes 786440 | tf_op jit(solution)/shard_map/ppermute | solution.py:265
  81.5 0.1 collective-permute-start.22
  81.6 2.9 %collective-permute-done.17 = bf16[32,4096]{1,0:T(8,128)(2,1)S(1)} collective-permute-done((bf16[32,4096]{1,0:T(8,128)(2,1)S(1)}, bf16[32,4096]{1,0:T(8,128)(2,1)S(1)}, u32[]{:S(2)}, u32[]{:S(2)}) %collective-permute-start.17) | collective-permute-done | bytes 262176 | tf_op jit(solution)/shard_map/ppermute | solution.py:265
  84.5 2.4 %collective-permute-start.25 = (bf16[32,4096]{1,0:T(8,128)(2,1)S(1)}, bf16[32,4096]{1,0:T(8,128)(2,1)S(1)}, u32[]{:S(2)}, u32[]{:S(2)}) collective-permute-start(bf16[32,4096]{1,0:T(8,128)(2,1)S(1)} %fusion.10), channel_id=1, source_target_pairs={{0,4},{4,8},{8,12},{12,14},{14,10},{10,6},{6,2},{2,0},{1,5},{5,9},... | collective-permute-start | bytes 786440 | tf_op jit(solution)/shard_map/ppermute | solution.py:265
  86.9 0.1 fusion.11
  87.0 0.1 collective-permute-start.24
  87.0 5.2 %shard_map.81 = f32[192,4096]{1,0:T(8,128)S(1)} custom-call(s32[448]{0:T(512)S(1)} %broadcast_add_fusion.2.refs_11_.rows, s32[225]{0:T(256)S(1)} %minimum_select_fusion.2.refs_12_.columns, f32[192,3584]{1,0:T(8,128)S(1)} %get-tuple-element.61.refs_0_, f32[192,3584]{1,0:T(8,128)S(1)} %collective-permute-done.2.refs_1_, ...), custom_call_target="tpu_custom_call" | custom-call | flops 2818572288 | bytes 14680064 | tf_op jit(solution)/shard_map/pallas_call | solution.py:229
  92.3 0.1 fusion.5
  92.3 2.5 %collective-permute-start.21 = (bf16[32,4096]{1,0:T(8,128)(2,1)S(1)}, bf16[32,4096]{1,0:T(8,128)(2,1)S(1)}, u32[]{:S(2)}, u32[]{:S(2)}) collective-permute-start(bf16[32,4096]{1,0:T(8,128)(2,1)S(1)} %fusion.5), channel_id=1, source_target_pairs={{0,4},{4,8},{8,12},{12,14},{14,10},{10,6},{6,2},{2,0},{1,5},{5,9},... | collective-permute-start | bytes 786440 | tf_op jit(solution)/shard_map/ppermute | solution.py:265
  94.9 0.7 collective-permute-done.25
  95.7 0.1 fusion.2
  95.7 2.4 %collective-permute-start.26 = (bf16[32,4096]{1,0:T(8,128)(2,1)S(1)}, bf16[32,4096]{1,0:T(8,128)(2,1)S(1)}, u32[]{:S(2)}, u32[]{:S(2)}) collective-permute-start(bf16[32,4096]{1,0:T(8,128)(2,1)S(1)} %fusion.2), channel_id=1, source_target_pairs={{0,4},{4,8},{8,12},{12,14},{14,10},{10,6},{6,2},{2,0},{1,5},{5,9},... | collective-permute-start | bytes 786440 | tf_op jit(solution)/shard_map/ppermute | solution.py:265
  98.1 0.1 fusion.3
  98.2 0.1 collective-permute-start.27
  98.3 5.4 %collective-permute-done.23 = bf16[32,4096]{1,0:T(8,128)(2,1)S(1)} collective-permute-done((bf16[32,4096]{1,0:T(8,128)(2,1)S(1)}, bf16[32,4096]{1,0:T(8,128)(2,1)S(1)}, u32[]{:S(2)}, u32[]{:S(2)}) %collective-permute-start.23) | collective-permute-done | bytes 262176 | tf_op jit(solution)/shard_map/ppermute | solution.py:265
  103.7 0.1 fusion.7
  103.8 2.7 %collective-permute-done.27 = bf16[32,4096]{1,0:T(8,128)(2,1)S(1)} collective-permute-done((bf16[32,4096]{1,0:T(8,128)(2,1)S(1)}, bf16[32,4096]{1,0:T(8,128)(2,1)S(1)}, u32[]{:S(2)}, u32[]{:S(2)}) %collective-permute-start.27) | collective-permute-done | bytes 262176 | tf_op jit(solution)/shard_map/ppermute | solution.py:265
  106.5 0.1 fusion.1
  106.6 0.8 pad_maximum_fusion
  (61 shorter events, 0.9 us)
Async XLA Ops:
  0.0 15.1 %collective-permute-start = (bf16[64,4096]{1,0:T(8,128)(2,1)}, bf16[64,4096]{1,0:T(8,128)(2,1)S(1)}, u32[]{:S(2)}, u32[]{:S(2)}) collective-permute-start(bf16[64,4096]{1,0:T(8,128)(2,1)} %refs_4_.3), channel_id=1, source_target_pairs={{0,4},{4,8},{8,12},{12,14},{14,10},{10,6},{6,2},{2,0},{1,5},{5,9},... | collective-permute-start | bytes 1572872 | tf_op jit(solution)/shard_map/ppermute | solution.py:321
  3.0 13.9 %collective-permute-start.1 = (bf16[64,4096]{1,0:T(8,128)(2,1)}, bf16[64,4096]{1,0:T(8,128)(2,1)S(1)}, u32[]{:S(2)}, u32[]{:S(2)}) collective-permute-start(bf16[64,4096]{1,0:T(8,128)(2,1)} %refs_4_.3), channel_id=1, source_target_pairs={{4,0},{8,4},{12,8},{14,12},{10,14},{6,10},{2,6},{0,2},{5,1},{9,5},... | collective-permute-start | bytes 1572872 | tf_op jit(solution)/shard_map/ppermute | solution.py:321
  7.3 9.9 %copy-start = (bf16[64,4096]{1,0:T(8,128)(2,1)S(1)}, bf16[64,4096]{1,0:T(8,128)(2,1)}, u32[]{:S(2)}) copy-start(bf16[64,4096]{1,0:T(8,128)(2,1)} %refs_4_.3) | copy-start | bytes 1572868
  15.1 14.9 %collective-permute-start.3 = (bf16[64,4096]{1,0:T(8,128)(2,1)S(1)}, bf16[64,4096]{1,0:T(8,128)(2,1)S(1)}, u32[]{:S(2)}, u32[]{:S(2)}) collective-permute-start(bf16[64,4096]{1,0:T(8,128)(2,1)S(1)} %collective-permute-done.refs_5_), channel_id=1, source_target_pairs={{0,4},{4,8},{8,12},{12,14},{14,10},{10,6},{6,2},{2,0},{1,5},{5,9},... | collective-permute-start | bytes 1572872 | tf_op jit(solution)/shard_map/ppermute | solution.py:321
  16.9 12.5 %collective-permute-start.4 = (bf16[64,4096]{1,0:T(8,128)(2,1)S(1)}, bf16[64,4096]{1,0:T(8,128)(2,1)S(1)}, u32[]{:S(2)}, u32[]{:S(2)}) collective-permute-start(bf16[64,4096]{1,0:T(8,128)(2,1)S(1)} %collective-permute-done.1.refs_6_), channel_id=1, source_target_pairs={{4,0},{8,4},{12,8},{14,12},{10,14},{6,10},{2,6},{0,2},{5,1},{9,5},... | collective-permute-start | bytes 1572872 | tf_op jit(solution)/shard_map/ppermute | solution.py:321
  25.6 31.2 %collective-permute-start.2 = (f32[192,3584]{1,0:T(8,128)S(1)}, f32[192,3584]{1,0:T(8,128)S(1)}, u32[]{:S(2)}, u32[]{:S(2)}) collective-permute-start(f32[192,3584]{1,0:T(8,128)S(1)} %get-tuple-element.61.refs_0_), channel_id=1, source_target_pairs={{0,1},{1,0},{2,3},{3,2},{4,5},{5,4},{6,7},{7,6},{8,9},{9,8},{10,11... | collective-permute-start | bytes 8257544 | tf_op jit(solution)/shard_map/ppermute | solution.py:304
  29.4 11.6 %collective-permute-start.7 = (bf16[64,4096]{1,0:T(8,128)(2,1)S(1)}, bf16[64,4096]{1,0:T(8,128)(2,1)S(1)}, u32[]{:S(2)}, u32[]{:S(2)}) collective-permute-start(bf16[64,4096]{1,0:T(8,128)(2,1)S(1)} %collective-permute-done.4.refs_5_), channel_id=1, source_target_pairs={{4,0},{8,4},{12,8},{14,12},{10,14},{6,10},{2,6},{0,2},{5,1},{9,5},... | collective-permute-start | bytes 1572872 | tf_op jit(solution)/shard_map/ppermute | solution.py:321
  30.0 12.1 %collective-permute-start.6 = (bf16[64,4096]{1,0:T(8,128)(2,1)S(1)}, bf16[64,4096]{1,0:T(8,128)(2,1)S(1)}, u32[]{:S(2)}, u32[]{:S(2)}) collective-permute-start(bf16[64,4096]{1,0:T(8,128)(2,1)S(1)} %collective-permute-done.3.refs_4_), channel_id=1, source_target_pairs={{0,4},{4,8},{8,12},{12,14},{14,10},{10,6},{6,2},{2,0},{1,5},{5,9},... | collective-permute-start | bytes 1572872 | tf_op jit(solution)/shard_map/ppermute | solution.py:321
  37.6 19.2 %collective-permute-start.5 = (f32[128,3584]{1,0:T(8,128)S(1)}, f32[128,3584]{1,0:T(8,128)S(1)}, u32[]{:S(2)}, u32[]{:S(2)}) collective-permute-start(f32[128,3584]{1,0:T(8,128)S(1)} %shard_map.75.refs_0_), channel_id=1, source_target_pairs={{0,1},{1,0},{2,3},{3,2},{4,5},{5,4},{6,7},{7,6},{8,9},{9,8},{10,11... | collective-permute-start | bytes 5505032 | tf_op jit(solution)/shard_map/ppermute | solution.py:304
  41.0 8.3 %collective-permute-start.10 = (bf16[64,2048]{1,0:T(8,128)(2,1)S(1)}, bf16[64,2048]{1,0:T(8,128)(2,1)S(1)}, u32[]{:S(2)}, u32[]{:S(2)}) collective-permute-start(bf16[64,2048]{1,0:T(8,128)(2,1)S(1)} %slice.112), channel_id=1, source_target_pairs={{4,0},{8,4},{12,8},{14,12},{10,14},{6,10},{2,6},{0,2},{5,1},{9,5},... | collective-permute-start | bytes 786440 | tf_op jit(solution)/shard_map/ppermute | solution.py:321
  42.1 7.3 %collective-permute-start.9 = (bf16[64,2048]{1,0:T(8,128)(2,1)S(1)}, bf16[64,2048]{1,0:T(8,128)(2,1)S(1)}, u32[]{:S(2)}, u32[]{:S(2)}) collective-permute-start(bf16[64,2048]{1,0:T(8,128)(2,1)S(1)} %slice.111), channel_id=1, source_target_pairs={{0,4},{4,8},{8,12},{12,14},{14,10},{10,6},{6,2},{2,0},{1,5},{5,9},... | collective-permute-start | bytes 786440 | tf_op jit(solution)/shard_map/ppermute | solution.py:321
  54.3 2.5 %collective-permute-start.11 = (f32[64,3584]{1,0:T(8,128)S(1)}, f32[64,3584]{1,0:T(8,128)S(1)}, u32[]{:S(2)}, u32[]{:S(2)}) collective-permute-start(f32[64,3584]{1,0:T(8,128)S(1)} %shard_map.78.refs_0_), channel_id=1, source_target_pairs={{0,1},{1,0},{2,3},{3,2},{4,5},{5,4},{6,7},{7,6},{8,9},{9,8},{10,11... | collective-permute-start | bytes 2752520 | tf_op jit(solution)/shard_map/ppermute | solution.py:304
  54.4 10.9 %collective-permute-start.8 = (f32[128,3584]{1,0:T(8,128)S(1)}, f32[128,3584]{1,0:T(8,128)S(1)}, u32[]{:S(2)}, u32[]{:S(2)}) collective-permute-start(f32[128,3584]{1,0:T(8,128)S(1)} %shard_map.76.refs_0_), channel_id=1, source_target_pairs={{0,1},{1,0},{2,3},{3,2},{4,5},{5,4},{6,7},{7,6},{8,9},{9,8},{10,11... | collective-permute-start | bytes 5505032 | tf_op jit(solution)/shard_map/ppermute | solution.py:304
  60.0 9.5 %collective-permute-start.15 = (bf16[32,2048]{1,0:T(8,128)(2,1)S(1)}, bf16[32,2048]{1,0:T(8,128)(2,1)S(1)}, u32[]{:S(2)}, u32[]{:S(2)}) collective-permute-start(bf16[32,2048]{1,0:T(8,128)(2,1)S(1)} %get-tuple-element.91), channel_id=1, source_target_pairs={{0,4},{4,8},{8,12},{12,14},{14,10},{10,6},{6,2},{2,0},{1,5},{5,9},... | collective-permute-start | bytes 393224 | tf_op jit(solution)/shard_map/ppermute | solution.py:265
  63.1 8.8 %collective-permute-start.14 = (bf16[32,2048]{1,0:T(8,128)(2,1)S(1)}, bf16[32,2048]{1,0:T(8,128)(2,1)S(1)}, u32[]{:S(2)}, u32[]{:S(2)}) collective-permute-start(bf16[32,2048]{1,0:T(8,128)(2,1)S(1)} %get-tuple-element.93), channel_id=1, source_target_pairs={{4,0},{8,4},{12,8},{14,12},{10,14},{6,10},{2,6},{0,2},{5,1},{9,5},... | collective-permute-start | bytes 393224 | tf_op jit(solution)/shard_map/ppermute | solution.py:265
  63.2 8.9 %collective-permute-start.13 = (bf16[32,2048]{1,0:T(8,128)(2,1)S(1)}, bf16[32,2048]{1,0:T(8,128)(2,1)S(1)}, u32[]{:S(2)}, u32[]{:S(2)}) collective-permute-start(bf16[32,2048]{1,0:T(8,128)(2,1)S(1)} %get-tuple-element.92), channel_id=1, source_target_pairs={{0,4},{4,8},{8,12},{12,14},{14,10},{10,6},{6,2},{2,0},{1,5},{5,9},... | collective-permute-start | bytes 393224 | tf_op jit(solution)/shard_map/ppermute | solution.py:265
  65.2 9.0 %collective-permute-start.12 = (bf16[32,2048]{1,0:T(8,128)(2,1)S(1)}, bf16[32,2048]{1,0:T(8,128)(2,1)S(1)}, u32[]{:S(2)}, u32[]{:S(2)}) collective-permute-start(bf16[32,2048]{1,0:T(8,128)(2,1)S(1)} %get-tuple-element.94), channel_id=1, source_target_pairs={{4,0},{8,4},{12,8},{14,12},{10,14},{6,10},{2,6},{0,2},{5,1},{9,5},... | collective-permute-start | bytes 393224 | tf_op jit(solution)/shard_map/ppermute | solution.py:265
  69.6 9.3 %collective-permute-start.19 = (bf16[32,4096]{1,0:T(8,128)(2,1)S(1)}, bf16[32,4096]{1,0:T(8,128)(2,1)S(1)}, u32[]{:S(2)}, u32[]{:S(2)}) collective-permute-start(bf16[32,4096]{1,0:T(8,128)(2,1)S(1)} %pad_maximum_fusion.1), channel_id=1, source_target_pairs={{0,4},{4,8},{8,12},{12,14},{14,10},{10,6},{6,2},{2,0},{1,5},{5,9},... | collective-permute-start | bytes 786440 | tf_op jit(solution)/shard_map/ppermute | solution.py:265
  72.0 9.5 %collective-permute-start.18 = (bf16[32,4096]{1,0:T(8,128)(2,1)S(1)}, bf16[32,4096]{1,0:T(8,128)(2,1)S(1)}, u32[]{:S(2)}, u32[]{:S(2)}) collective-permute-start(bf16[32,4096]{1,0:T(8,128)(2,1)S(1)} %pad_maximum_fusion.2), channel_id=1, source_target_pairs={{4,0},{8,4},{12,8},{14,12},{10,14},{6,10},{2,6},{0,2},{5,1},{9,5},... | collective-permute-start | bytes 786440 | tf_op jit(solution)/shard_map/ppermute | solution.py:265
  72.1 12.3 %collective-permute-start.17 = (bf16[32,4096]{1,0:T(8,128)(2,1)S(1)}, bf16[32,4096]{1,0:T(8,128)(2,1)S(1)}, u32[]{:S(2)}, u32[]{:S(2)}) collective-permute-start(bf16[32,4096]{1,0:T(8,128)(2,1)S(1)} %pad_maximum_fusion.3), channel_id=1, source_target_pairs={{0,4},{4,8},{8,12},{12,14},{14,10},{10,6},{6,2},{2,0},{1,5},{5,9},... | collective-permute-start | bytes 786440 | tf_op jit(solution)/shard_map/ppermute | solution.py:265
  74.2 12.7 %collective-permute-start.16 = (bf16[32,4096]{1,0:T(8,128)(2,1)S(1)}, bf16[32,4096]{1,0:T(8,128)(2,1)S(1)}, u32[]{:S(2)}, u32[]{:S(2)}) collective-permute-start(bf16[32,4096]{1,0:T(8,128)(2,1)S(1)} %pad_maximum_fusion.4), channel_id=1, source_target_pairs={{4,0},{8,4},{12,8},{14,12},{10,14},{6,10},{2,6},{0,2},{5,1},{9,5},... | collective-permute-start | bytes 786440 | tf_op jit(solution)/shard_map/ppermute | solution.py:265
  78.9 13.4 %collective-permute-start.20 = (bf16[32,4096]{1,0:T(8,128)(2,1)S(1)}, bf16[32,4096]{1,0:T(8,128)(2,1)S(1)}, u32[]{:S(2)}, u32[]{:S(2)}) collective-permute-start(bf16[32,4096]{1,0:T(8,128)(2,1)S(1)} %fusion.8), channel_id=1, source_target_pairs={{0,4},{4,8},{8,12},{12,14},{14,10},{10,6},{6,2},{2,0},{1,5},{5,9},... | collective-permute-start | bytes 786440 | tf_op jit(solution)/shard_map/ppermute | solution.py:265
  81.5 13.3 %collective-permute-start.22 = (bf16[32,4096]{1,0:T(8,128)(2,1)S(1)}, bf16[32,4096]{1,0:T(8,128)(2,1)S(1)}, u32[]{:S(2)}, u32[]{:S(2)}) collective-permute-start(bf16[32,4096]{1,0:T(8,128)(2,1)S(1)} %fusion.9), channel_id=1, source_target_pairs={{4,0},{8,4},{12,8},{14,12},{10,14},{6,10},{2,6},{0,2},{5,1},{9,5},... | collective-permute-start | bytes 786440 | tf_op jit(solution)/shard_map/ppermute | solution.py:265
  84.5 11.2 %collective-permute-start.25 = (bf16[32,4096]{1,0:T(8,128)(2,1)S(1)}, bf16[32,4096]{1,0:T(8,128)(2,1)S(1)}, u32[]{:S(2)}, u32[]{:S(2)}) collective-permute-start(bf16[32,4096]{1,0:T(8,128)(2,1)S(1)} %fusion.10), channel_id=1, source_target_pairs={{0,4},{4,8},{8,12},{12,14},{14,10},{10,6},{6,2},{2,0},{1,5},{5,9},... | collective-permute-start | bytes 786440 | tf_op jit(solution)/shard_map/ppermute | solution.py:265
  87.0 11.2 %collective-permute-start.24 = (bf16[32,4096]{1,0:T(8,128)(2,1)S(1)}, bf16[32,4096]{1,0:T(8,128)(2,1)S(1)}, u32[]{:S(2)}, u32[]{:S(2)}) collective-permute-start(bf16[32,4096]{1,0:T(8,128)(2,1)S(1)} %fusion.11), channel_id=1, source_target_pairs={{4,0},{8,4},{12,8},{14,12},{10,14},{6,10},{2,6},{0,2},{5,1},{9,5},... | collective-permute-start | bytes 786440 | tf_op jit(solution)/shard_map/ppermute | solution.py:265
  92.3 11.4 %collective-permute-start.21 = (bf16[32,4096]{1,0:T(8,128)(2,1)S(1)}, bf16[32,4096]{1,0:T(8,128)(2,1)S(1)}, u32[]{:S(2)}, u32[]{:S(2)}) collective-permute-start(bf16[32,4096]{1,0:T(8,128)(2,1)S(1)} %fusion.5), channel_id=1, source_target_pairs={{0,4},{4,8},{8,12},{12,14},{14,10},{10,6},{6,2},{2,0},{1,5},{5,9},... | collective-permute-start | bytes 786440 | tf_op jit(solution)/shard_map/ppermute | solution.py:265
  94.9 8.8 %collective-permute-start.23 = (bf16[32,4096]{1,0:T(8,128)(2,1)S(1)}, bf16[32,4096]{1,0:T(8,128)(2,1)S(1)}, u32[]{:S(2)}, u32[]{:S(2)}) collective-permute-start(bf16[32,4096]{1,0:T(8,128)(2,1)S(1)} %fusion.4), channel_id=1, source_target_pairs={{4,0},{8,4},{12,8},{14,12},{10,14},{6,10},{2,6},{0,2},{5,1},{9,5},... | collective-permute-start | bytes 786440 | tf_op jit(solution)/shard_map/ppermute | solution.py:265
  95.7 10.8 %collective-permute-start.26 = (bf16[32,4096]{1,0:T(8,128)(2,1)S(1)}, bf16[32,4096]{1,0:T(8,128)(2,1)S(1)}, u32[]{:S(2)}, u32[]{:S(2)}) collective-permute-start(bf16[32,4096]{1,0:T(8,128)(2,1)S(1)} %fusion.2), channel_id=1, source_target_pairs={{0,4},{4,8},{8,12},{12,14},{14,10},{10,6},{6,2},{2,0},{1,5},{5,9},... | collective-permute-start | bytes 786440 | tf_op jit(solution)/shard_map/ppermute | solution.py:265
  98.2 8.3 %collective-permute-start.27 = (bf16[32,4096]{1,0:T(8,128)(2,1)S(1)}, bf16[32,4096]{1,0:T(8,128)(2,1)S(1)}, u32[]{:S(2)}, u32[]{:S(2)}) collective-permute-start(bf16[32,4096]{1,0:T(8,128)(2,1)S(1)} %fusion.3), channel_id=1, source_target_pairs={{4,0},{8,4},{12,8},{14,12},{10,14},{6,10},{2,6},{0,2},{5,1},{9,5},... | collective-permute-start | bytes 786440 | tf_op jit(solution)/shard_map/ppermute | solution.py:265

commit v3 on v2

--- a/solution.py
+++ b/solution.py
@@ -9,7 +9,7 @@
 
 SIDE = 128
 DEPTH = 2
-ITEMS = 8
+ITEMS = 20
 TRIP = ITEMS * DEPTH
 HELD = 2
 F32 = jnp.float32

time: 108 us -> 103 us (0.954); the launches traced: 107 us -> 104 us
  Pallas kernels: 46.7 us -> 34.6 us
  waiting for transfers between devices: 24.4 us -> 34 us
  starting transfers between devices: 29.7 us -> 28.4 us
    pallas_call x4, Pallas kernels: 25.7 us -> 18 us  [tokens_product(): pl.pallas_call(functools.partial(tokens_kernel, places, bool(to_pack)), o...]
    ppermute x16, waiting for transfers between devices: 12.3 us -> 16.9 us  [scatter(): lax.ppermute(block, 'row', way)]
    ppermute x4, waiting for transfers between devices: 7.07 us -> 11.6 us  [body(): lax.ppermute(ahead, 'row', back)]
    pallas_call x4, Pallas kernels: 16.4 us -> 11.9 us  [down_product(): pl.pallas_call(functools.partial(down_kernel, groups, opposite), out_shap...]
    ppermute x16, starting transfers between devices: 19.8 us -> 18.5 us  [scatter(): lax.ppermute(block, 'row', way)]
  transfers between devices with their start and end apart: 28 -> 28, of which waited for: 9 -> 13; matrix products, arithmetic and copies ran while one was open for 5% -> 5% of each run, Pallas kernels for 43% -> 33%
where the time goes in v3:
time: 103 us; the launch traced here: 104 us
  Pallas kernels  34.6 us (34%)
  waiting for transfers between devices  34 us (33%)
  starting transfers between devices  28.4 us (28%)
  other arithmetic  6.07 us (6%)
    ppermute x16, starting transfers between devices, scatter(): lax.ppermute(block, 'row', way)  18.5 us
    pallas_call x4, Pallas kernels, tokens_product(): pl.pallas_call(functools.partial(tokens_kernel, places, bool(to_pack)), o...  18 us
    ppermute x16, waiting for transfers between devices, scatter(): lax.ppermute(block, 'row', way)  16.9 us
    pallas_call x4, Pallas kernels, down_product(): pl.pallas_call(functools.partial(down_kernel, groups, opposite), out_shap...  11.9 us
    ppermute x4, waiting for transfers between devices, body(): lax.ppermute(ahead, 'row', back)  11.6 us
    ppermute x4, starting transfers between devices, body(): lax.ppermute(behind, 'row', onward)  7.84 us
    pallas_call x1, Pallas kernels, pack(): pl.pallas_call(functools.partial(pack_kernel, count), out_shape=[packed_s...  4.69 us
    ppermute x4, waiting for transfers between devices, body(): lax.ppermute(behind, 'row', onward)  3.54 us
  transfers between devices with their start and end apart: 28, of which 13 were waited for; matrix products, arithmetic and copies ran while one was open for 5% of the time, Pallas kernels for 33%

profile of v3, /device:TPU:0, one launch (start us, length us, event | category | flops | bytes accessed | tf_op | source)
XLA Modules:
  0.0 103.6 jit_solution(4065767091777172845)
XLA Ops:
  0.0 3.0 %collective-permute-start = (bf16[64,4096]{1,0:T(8,128)(2,1)}, bf16[64,4096]{1,0:T(8,128)(2,1)S(1)}, u32[]{:S(2)}, u32[]{:S(2)}) collective-permute-start(bf16[64,4096]{1,0:T(8,128)(2,1)} %refs_4_.3), channel_id=1, source_target_pairs={{0,4},{4,8},{8,12},{12,14},{14,10},{10,6},{6,2},{2,0},{1,5},{5,9},... | collective-permute-start | bytes 1572872 | tf_op jit(solution)/shard_map/ppermute | solution.py:321
  3.1 0.8 convert_reduce_fusion.3
  3.9 0.8 convert_reduce_fusion.4
  4.7 0.1 select_reduce_fusion.8
  4.9 0.1 select_reduce_fusion.7
  5.0 0.5 select_reduce_fusion.3
  5.6 0.1 add_select_fusion
  5.6 0.3 select_reduce_fusion
  6.0 0.1 convert_reduce_fusion.1
  6.0 0.7 convert_reduce_fusion.5
  6.8 0.1 select_reduce_fusion.6
  6.9 0.1 select_reduce_fusion.5
  7.1 0.2 select_reduce_fusion.2
  7.3 4.7 %shard_map.73 = (bf16[30720,128]{1,0:T(8,128)(2,1)S(1)}, bf16[30720,128]{1,0:T(8,128)(2,1)S(1)}) custom-call(s32[480]{0:T(512)S(1)} %broadcast_add_fusion.1.refs_0_, s32[241]{0:T(256)S(1)} %get-tuple-element.98.refs_1_, s32[480]{0:T(512)S(1)} %broadcast_add_fusion.refs_2_, s32[241]{0:T(256)S(1)} %get-tuple-element.97.refs_3_, bf16[4096,1792]{1,0:T(8,128)(2,1)} %refs_8_.5, ...), custom_call_target="tpu_custom_call" | custom-call | bytes 29360128 | tf_op jit(solution)/shard_map/pallas_call | solution.py:136
  12.0 0.1 add_reduce_fusion
  12.1 3.0 %collective-permute-done.refs_5_ = bf16[64,4096]{1,0:T(8,128)(2,1)S(1)} collective-permute-done((bf16[64,4096]{1,0:T(8,128)(2,1)}, bf16[64,4096]{1,0:T(8,128)(2,1)S(1)}, u32[]{:S(2)}, u32[]{:S(2)}) %collective-permute-start) | collective-permute-done | bytes 524320 | tf_op jit(solution)/shard_map/ppermute | solution.py:321
  15.1 1.8 %collective-permute-start.3 = (bf16[64,4096]{1,0:T(8,128)(2,1)S(1)}, bf16[64,4096]{1,0:T(8,128)(2,1)S(1)}, u32[]{:S(2)}, u32[]{:S(2)}) collective-permute-start(bf16[64,4096]{1,0:T(8,128)(2,1)S(1)} %collective-permute-done.refs_5_), channel_id=1, source_target_pairs={{0,4},{4,8},{8,12},{12,14},{14,10},{10,6},{6,2},{2,0},{1,5},{5,9},... | collective-permute-start | bytes 1572872 | tf_op jit(solution)/shard_map/ppermute | solution.py:321
  16.9 0.2 collective-permute-start.4
  17.1 6.2 %shard_map.74 = (f32[192,3584]{1,0:T(8,128)S(1)}, bf16[30720,128]{1,0:T(8,128)(2,1)S(1)}) custom-call(s32[480]{0:T(512)S(1)} %broadcast_add_fusion.1.refs_0_, s32[241]{0:T(256)S(1)} %get-tuple-element.98.refs_1_, s32[480]{0:T(512)S(1)} %broadcast_add_fusion.refs_2_, s32[241]{0:T(256)S(1)} %get-tuple-element.97.refs_3_, bf16[64,4096]{1,0:T(8,128)(2,1)S(1)} %copy-done, ...), custom_call_target="tpu_custom_call" | custom-call | flops 22548578304 | bytes 117440512 | tf_op jit(solution)/shard_map/pallas_call | solution.py:180
  23.3 0.1 collective-permute-start.2
  23.4 6.0 %collective-permute-done.4.refs_5_ = bf16[64,4096]{1,0:T(8,128)(2,1)S(1)} collective-permute-done((bf16[64,4096]{1,0:T(8,128)(2,1)S(1)}, bf16[64,4096]{1,0:T(8,128)(2,1)S(1)}, u32[]{:S(2)}, u32[]{:S(2)}) %collective-permute-start.4) | collective-permute-done | bytes 524320 | tf_op jit(solution)/shard_map/ppermute | solution.py:321
  29.4 0.5 collective-permute-start.7
  30.0 1.5 %collective-permute-start.6 = (bf16[64,4096]{1,0:T(8,128)(2,1)S(1)}, bf16[64,4096]{1,0:T(8,128)(2,1)S(1)}, u32[]{:S(2)}, u32[]{:S(2)}) collective-permute-start(bf16[64,4096]{1,0:T(8,128)(2,1)S(1)} %collective-permute-done.3.refs_4_), channel_id=1, source_target_pairs={{0,4},{4,8},{8,12},{12,14},{14,10},{10,6},{6,2},{2,0},{1,5},{5,9},... | collective-permute-start | bytes 1572872 | tf_op jit(solution)/shard_map/ppermute | solution.py:321
  31.4 4.3 %shard_map.75.refs_0_ = f32[128,3584]{1,0:T(8,128)S(1)} custom-call(s32[480]{0:T(512)S(1)} %broadcast_add_fusion.1.refs_0_, s32[241]{0:T(256)S(1)} %get-tuple-element.98.refs_1_, s32[480]{0:T(512)S(1)} %broadcast_add_fusion.refs_2_, s32[241]{0:T(256)S(1)} %get-tuple-element.97.refs_3_, bf16[64,4096]{1,0:T(8,128)(2,1)S(1)} %collective-permute-done.3.refs_4_, ...), custom_call_target="tpu_custom_call" | custom-call | flops 15032385536 | bytes 117440512 | tf_op jit(solution)/shard_map/pallas_call | solution.py:180
  35.8 0.1 collective-permute-start.5
  35.9 5.6 %collective-permute-done.7.refs_5_ = bf16[64,4096]{1,0:T(8,128)(2,1)S(1)} collective-permute-done((bf16[64,4096]{1,0:T(8,128)(2,1)S(1)}, bf16[64,4096]{1,0:T(8,128)(2,1)S(1)}, u32[]{:S(2)}, u32[]{:S(2)}) %collective-permute-start.7) | collective-permute-done | bytes 524320 | tf_op jit(solution)/shard_map/ppermute | solution.py:321
  41.5 0.6 collective-permute-start.10
  42.1 1.5 %collective-permute-start.9 = (bf16[64,2048]{1,0:T(8,128)(2,1)S(1)}, bf16[64,2048]{1,0:T(8,128)(2,1)S(1)}, u32[]{:S(2)}, u32[]{:S(2)}) collective-permute-start(bf16[64,2048]{1,0:T(8,128)(2,1)S(1)} %slice.111), channel_id=1, source_target_pairs={{0,4},{4,8},{8,12},{12,14},{14,10},{10,6},{6,2},{2,0},{1,5},{5,9},... | collective-permute-start | bytes 786440 | tf_op jit(solution)/shard_map/ppermute | solution.py:321
  43.6 4.3 %shard_map.76.refs_0_ = f32[128,3584]{1,0:T(8,128)S(1)} custom-call(s32[480]{0:T(512)S(1)} %broadcast_add_fusion.1.refs_0_, s32[241]{0:T(256)S(1)} %get-tuple-element.98.refs_1_, s32[480]{0:T(512)S(1)} %broadcast_add_fusion.refs_2_, s32[241]{0:T(256)S(1)} %get-tuple-element.97.refs_3_, bf16[64,4096]{1,0:T(8,128)(2,1)S(1)} %collective-permute-done.6.refs_4_, ...), custom_call_target="tpu_custom_call" | custom-call | flops 15032385536 | bytes 117440512 | tf_op jit(solution)/shard_map/pallas_call | solution.py:180
  47.9 0.6 collective-permute-done.9.refs_4_
  48.5 3.2 %shard_map.78.refs_0_ = f32[64,3584]{1,0:T(8,128)S(1)} custom-call(s32[480]{0:T(512)S(1)} %broadcast_add_fusion.1.refs_0_, s32[241]{0:T(256)S(1)} %get-tuple-element.98.refs_1_, s32[480]{0:T(512)S(1)} %broadcast_add_fusion.refs_2_, s32[241]{0:T(256)S(1)} %get-tuple-element.97.refs_3_, bf16[64,2048]{1,0:T(8,128)(2,1)S(1)} %collective-permute-done.9.refs_4_, ...), custom_call_target="tpu_custom_call" | custom-call | flops 7516192768 | bytes 117440512 | tf_op jit(solution)/shard_map/pallas_call | solution.py:180
  51.7 0.1 collective-permute-start.11
  51.8 0.5 collective-permute-start.8
  52.3 2.0 %collective-permute-done.11.refs_1_ = f32[64,3584]{1,0:T(8,128)S(1)} collective-permute-done((f32[64,3584]{1,0:T(8,128)S(1)}, f32[64,3584]{1,0:T(8,128)S(1)}, u32[]{:S(2)}, u32[]{:S(2)}) %collective-permute-start.11) | collective-permute-done | bytes 917536 | tf_op jit(solution)/shard_map/ppermute | solution.py:304
  54.2 2.0 %shard_map.79 = (bf16[64,2048]{1,0:T(8,128)(2,1)S(1)}, bf16[64,2048]{1,0:T(8,128)(2,1)S(1)}) custom-call(s32[480]{0:T(512)S(1)} %broadcast_add_fusion.2.refs_11_.rows, s32[241]{0:T(256)S(1)} %minimum_select_fusion.2.refs_12_.columns, f32[64,3584]{1,0:T(8,128)S(1)} %shard_map.78.refs_0_, f32[64,3584]{1,0:T(8,128)S(1)} %collective-permute-done.11.refs_1_, ...), custom_call_target="tpu_custom_call" | custom-call | flops 939524096 | bytes 14680064 | tf_op jit(solution)/shard_map/pallas_call | solution.py:229
  56.3 1.5 %collective-permute-start.15 = (bf16[32,2048]{1,0:T(8,128)(2,1)S(1)}, bf16[32,2048]{1,0:T(8,128)(2,1)S(1)}, u32[]{:S(2)}, u32[]{:S(2)}) collective-permute-start(bf16[32,2048]{1,0:T(8,128)(2,1)S(1)} %get-tuple-element.91), channel_id=1, source_target_pairs={{0,4},{4,8},{8,12},{12,14},{14,10},{10,6},{6,2},{2,0},{1,5},{5,9},... | collective-permute-start | bytes 393224 | tf_op jit(solution)/shard_map/ppermute | solution.py:265
  57.9 1.2 %collective-permute-start.14 = (bf16[32,2048]{1,0:T(8,128)(2,1)S(1)}, bf16[32,2048]{1,0:T(8,128)(2,1)S(1)}, u32[]{:S(2)}, u32[]{:S(2)}) collective-permute-start(bf16[32,2048]{1,0:T(8,128)(2,1)S(1)} %get-tuple-element.93), channel_id=1, source_target_pairs={{4,0},{8,4},{12,8},{14,12},{10,14},{6,10},{2,6},{0,2},{5,1},{9,5},... | collective-permute-start | bytes 393224 | tf_op jit(solution)/shard_map/ppermute | solution.py:265
  59.1 2.3 %collective-permute-start.13 = (bf16[32,2048]{1,0:T(8,128)(2,1)S(1)}, bf16[32,2048]{1,0:T(8,128)(2,1)S(1)}, u32[]{:S(2)}, u32[]{:S(2)}) collective-permute-start(bf16[32,2048]{1,0:T(8,128)(2,1)S(1)} %get-tuple-element.92), channel_id=1, source_target_pairs={{0,4},{4,8},{8,12},{12,14},{14,10},{10,6},{6,2},{2,0},{1,5},{5,9},... | collective-permute-start | bytes 393224 | tf_op jit(solution)/shard_map/ppermute | solution.py:265
  61.4 3.0 %shard_map.77 = f32[128,4096]{1,0:T(8,128)S(1)} custom-call(s32[480]{0:T(512)S(1)} %broadcast_add_fusion.2.refs_11_.rows, s32[241]{0:T(256)S(1)} %minimum_select_fusion.2.refs_12_.columns, f32[128,3584]{1,0:T(8,128)S(1)} %shard_map.76.refs_0_, f32[128,3584]{1,0:T(8,128)S(1)} %collective-permute-done.8.refs_1_, ...), custom_call_target="tpu_custom_call" | custom-call | flops 1879048192 | bytes 14680064 | tf_op jit(solution)/shard_map/pallas_call | solution.py:229
  64.4 0.1 convert.22
  64.6 2.0 %collective-permute-start.19 = (bf16[32,4096]{1,0:T(8,128)(2,1)S(1)}, bf16[32,4096]{1,0:T(8,128)(2,1)S(1)}, u32[]{:S(2)}, u32[]{:S(2)}) collective-permute-start(bf16[32,4096]{1,0:T(8,128)(2,1)S(1)} %pad_maximum_fusion.1), channel_id=1, source_target_pairs={{0,4},{4,8},{8,12},{12,14},{14,10},{10,6},{6,2},{2,0},{1,5},{5,9},... | collective-permute-start | bytes 786440 | tf_op jit(solution)/shard_map/ppermute | solution.py:265
  66.7 0.4 collective-permute-start.18
  67.2 2.3 %collective-permute-start.17 = (bf16[32,4096]{1,0:T(8,128)(2,1)S(1)}, bf16[32,4096]{1,0:T(8,128)(2,1)S(1)}, u32[]{:S(2)}, u32[]{:S(2)}) collective-permute-start(bf16[32,4096]{1,0:T(8,128)(2,1)S(1)} %pad_maximum_fusion.3), channel_id=1, source_target_pairs={{0,4},{4,8},{8,12},{12,14},{14,10},{10,6},{6,2},{2,0},{1,5},{5,9},... | collective-permute-start | bytes 786440 | tf_op jit(solution)/shard_map/ppermute | solution.py:265
  69.6 2.9 %shard_map.80 = f32[128,4096]{1,0:T(8,128)S(1)} custom-call(s32[480]{0:T(512)S(1)} %broadcast_add_fusion.2.refs_11_.rows, s32[241]{0:T(256)S(1)} %minimum_select_fusion.2.refs_12_.columns, f32[128,3584]{1,0:T(8,128)S(1)} %shard_map.75.refs_0_, f32[128,3584]{1,0:T(8,128)S(1)} %collective-permute-done.5.refs_1_, ...), custom_call_target="tpu_custom_call" | custom-call | flops 1879048192 | bytes 14680064 | tf_op jit(solution)/shard_map/pallas_call | solution.py:229
  72.5 1.6 %collective-permute-done.19 = bf16[32,4096]{1,0:T(8,128)(2,1)S(1)} collective-permute-done((bf16[32,4096]{1,0:T(8,128)(2,1)S(1)}, bf16[32,4096]{1,0:T(8,128)(2,1)S(1)}, u32[]{:S(2)}, u32[]{:S(2)}) %collective-permute-start.19) | collective-permute-done | bytes 262176 | tf_op jit(solution)/shard_map/ppermute | solution.py:265
  74.2 1.9 %collective-permute-start.20 = (bf16[32,4096]{1,0:T(8,128)(2,1)S(1)}, bf16[32,4096]{1,0:T(8,128)(2,1)S(1)}, u32[]{:S(2)}, u32[]{:S(2)}) collective-permute-start(bf16[32,4096]{1,0:T(8,128)(2,1)S(1)} %fusion.8), channel_id=1, source_target_pairs={{0,4},{4,8},{8,12},{12,14},{14,10},{10,6},{6,2},{2,0},{1,5},{5,9},... | collective-permute-start | bytes 786440 | tf_op jit(solution)/shard_map/ppermute | solution.py:265
  76.1 0.5 collective-permute-done.18
  76.7 3.0 %collective-permute-done.17 = bf16[32,4096]{1,0:T(8,128)(2,1)S(1)} collective-permute-done((bf16[32,4096]{1,0:T(8,128)(2,1)S(1)}, bf16[32,4096]{1,0:T(8,128)(2,1)S(1)}, u32[]{:S(2)}, u32[]{:S(2)}) %collective-permute-start.17) | collective-permute-done | bytes 262176 | tf_op jit(solution)/shard_map/ppermute | solution.py:265
  79.8 1.9 %collective-permute-start.25 = (bf16[32,4096]{1,0:T(8,128)(2,1)S(1)}, bf16[32,4096]{1,0:T(8,128)(2,1)S(1)}, u32[]{:S(2)}, u32[]{:S(2)}) collective-permute-start(bf16[32,4096]{1,0:T(8,128)(2,1)S(1)} %fusion.10), channel_id=1, source_target_pairs={{0,4},{4,8},{8,12},{12,14},{14,10},{10,6},{6,2},{2,0},{1,5},{5,9},... | collective-permute-start | bytes 786440 | tf_op jit(solution)/shard_map/ppermute | solution.py:265
  81.7 0.5 collective-permute-done.16
  82.2 0.1 fusion.11
  82.3 4.0 %shard_map.81 = f32[192,4096]{1,0:T(8,128)S(1)} custom-call(s32[480]{0:T(512)S(1)} %broadcast_add_fusion.2.refs_11_.rows, s32[241]{0:T(256)S(1)} %minimum_select_fusion.2.refs_12_.columns, f32[192,3584]{1,0:T(8,128)S(1)} %get-tuple-element.61.refs_0_, f32[192,3584]{1,0:T(8,128)S(1)} %collective-permute-done.2.refs_1_, ...), custom_call_target="tpu_custom_call" | custom-call | flops 2818572288 | bytes 14680064 | tf_op jit(solution)/shard_map/pallas_call | solution.py:229
  86.3 0.1 fusion.5
  86.4 2.0 %collective-permute-start.21 = (bf16[32,4096]{1,0:T(8,128)(2,1)S(1)}, bf16[32,4096]{1,0:T(8,128)(2,1)S(1)}, u32[]{:S(2)}, u32[]{:S(2)}) collective-permute-start(bf16[32,4096]{1,0:T(8,128)(2,1)S(1)} %fusion.5), channel_id=1, source_target_pairs={{0,4},{4,8},{8,12},{12,14},{14,10},{10,6},{6,2},{2,0},{1,5},{5,9},... | collective-permute-start | bytes 786440 | tf_op jit(solution)/shard_map/ppermute | solution.py:265
  88.5 0.7 collective-permute-start.23
  89.2 1.8 %collective-permute-done.25 = bf16[32,4096]{1,0:T(8,128)(2,1)S(1)} collective-permute-done((bf16[32,4096]{1,0:T(8,128)(2,1)S(1)}, bf16[32,4096]{1,0:T(8,128)(2,1)S(1)}, u32[]{:S(2)}, u32[]{:S(2)}) %collective-permute-start.25) | collective-permute-done | bytes 262176 | tf_op jit(solution)/shard_map/ppermute | solution.py:265
  91.0 1.9 %collective-permute-start.26 = (bf16[32,4096]{1,0:T(8,128)(2,1)S(1)}, bf16[32,4096]{1,0:T(8,128)(2,1)S(1)}, u32[]{:S(2)}, u32[]{:S(2)}) collective-permute-start(bf16[32,4096]{1,0:T(8,128)(2,1)S(1)} %fusion.2), channel_id=1, source_target_pairs={{0,4},{4,8},{8,12},{12,14},{14,10},{10,6},{6,2},{2,0},{1,5},{5,9},... | collective-permute-start | bytes 786440 | tf_op jit(solution)/shard_map/ppermute | solution.py:265
  93.0 0.5 collective-permute-done.24
  93.4 0.1 fusion.3
  93.5 5.5 %collective-permute-done.23 = bf16[32,4096]{1,0:T(8,128)(2,1)S(1)} collective-permute-done((bf16[32,4096]{1,0:T(8,128)(2,1)S(1)}, bf16[32,4096]{1,0:T(8,128)(2,1)S(1)}, u32[]{:S(2)}, u32[]{:S(2)}) %collective-permute-start.23) | collective-permute-done | bytes 262176 | tf_op jit(solution)/shard_map/ppermute | solution.py:265
  99.0 0.1 fusion.7
  99.1 3.6 %collective-permute-done.27 = bf16[32,4096]{1,0:T(8,128)(2,1)S(1)} collective-permute-done((bf16[32,4096]{1,0:T(8,128)(2,1)S(1)}, bf16[32,4096]{1,0:T(8,128)(2,1)S(1)}, u32[]{:S(2)}, u32[]{:S(2)}) %collective-permute-start.27) | collective-permute-done | bytes 262176 | tf_op jit(solution)/shard_map/ppermute | solution.py:265
  102.7 0.1 fusion.1
  102.8 0.8 pad_maximum_fusion
  (61 shorter events, 1.1 us)
Async XLA Ops:
  0.0 15.1 %collective-permute-start = (bf16[64,4096]{1,0:T(8,128)(2,1)}, bf16[64,4096]{1,0:T(8,128)(2,1)S(1)}, u32[]{:S(2)}, u32[]{:S(2)}) collective-permute-start(bf16[64,4096]{1,0:T(8,128)(2,1)} %refs_4_.3), channel_id=1, source_target_pairs={{0,4},{4,8},{8,12},{12,14},{14,10},{10,6},{6,2},{2,0},{1,5},{5,9},... | collective-permute-start | bytes 1572872 | tf_op jit(solution)/shard_map/ppermute | solution.py:321
  3.0 13.9 %collective-permute-start.1 = (bf16[64,4096]{1,0:T(8,128)(2,1)}, bf16[64,4096]{1,0:T(8,128)(2,1)S(1)}, u32[]{:S(2)}, u32[]{:S(2)}) collective-permute-start(bf16[64,4096]{1,0:T(8,128)(2,1)} %refs_4_.3), channel_id=1, source_target_pairs={{4,0},{8,4},{12,8},{14,12},{10,14},{6,10},{2,6},{0,2},{5,1},{9,5},... | collective-permute-start | bytes 1572872 | tf_op jit(solution)/shard_map/ppermute | solution.py:321
  7.3 9.9 %copy-start = (bf16[64,4096]{1,0:T(8,128)(2,1)S(1)}, bf16[64,4096]{1,0:T(8,128)(2,1)}, u32[]{:S(2)}) copy-start(bf16[64,4096]{1,0:T(8,128)(2,1)} %refs_4_.3) | copy-start | bytes 1572868
  15.1 14.9 %collective-permute-start.3 = (bf16[64,4096]{1,0:T(8,128)(2,1)S(1)}, bf16[64,4096]{1,0:T(8,128)(2,1)S(1)}, u32[]{:S(2)}, u32[]{:S(2)}) collective-permute-start(bf16[64,4096]{1,0:T(8,128)(2,1)S(1)} %collective-permute-done.refs_5_), channel_id=1, source_target_pairs={{0,4},{4,8},{8,12},{12,14},{14,10},{10,6},{6,2},{2,0},{1,5},{5,9},... | collective-permute-start | bytes 1572872 | tf_op jit(solution)/shard_map/ppermute | solution.py:321
  16.9 12.5 %collective-permute-start.4 = (bf16[64,4096]{1,0:T(8,128)(2,1)S(1)}, bf16[64,4096]{1,0:T(8,128)(2,1)S(1)}, u32[]{:S(2)}, u32[]{:S(2)}) collective-permute-start(bf16[64,4096]{1,0:T(8,128)(2,1)S(1)} %collective-permute-done.1.refs_6_), channel_id=1, source_target_pairs={{4,0},{8,4},{12,8},{14,12},{10,14},{6,10},{2,6},{0,2},{5,1},{9,5},... | collective-permute-start | bytes 1572872 | tf_op jit(solution)/shard_map/ppermute | solution.py:321
  23.3 30.9 %collective-permute-start.2 = (f32[192,3584]{1,0:T(8,128)S(1)}, f32[192,3584]{1,0:T(8,128)S(1)}, u32[]{:S(2)}, u32[]{:S(2)}) collective-permute-start(f32[192,3584]{1,0:T(8,128)S(1)} %get-tuple-element.61.refs_0_), channel_id=1, source_target_pairs={{0,1},{1,0},{2,3},{3,2},{4,5},{5,4},{6,7},{7,6},{8,9},{9,8},{10,11... | collective-permute-start | bytes 8257544 | tf_op jit(solution)/shard_map/ppermute | solution.py:304
  29.4 12.0 %collective-permute-start.7 = (bf16[64,4096]{1,0:T(8,128)(2,1)S(1)}, bf16[64,4096]{1,0:T(8,128)(2,1)S(1)}, u32[]{:S(2)}, u32[]{:S(2)}) collective-permute-start(bf16[64,4096]{1,0:T(8,128)(2,1)S(1)} %collective-permute-done.4.refs_5_), channel_id=1, source_target_pairs={{4,0},{8,4},{12,8},{14,12},{10,14},{6,10},{2,6},{0,2},{5,1},{9,5},... | collective-permute-start | bytes 1572872 | tf_op jit(solution)/shard_map/ppermute | solution.py:321
  30.0 12.1 %collective-permute-start.6 = (bf16[64,4096]{1,0:T(8,128)(2,1)S(1)}, bf16[64,4096]{1,0:T(8,128)(2,1)S(1)}, u32[]{:S(2)}, u32[]{:S(2)}) collective-permute-start(bf16[64,4096]{1,0:T(8,128)(2,1)S(1)} %collective-permute-done.3.refs_4_), channel_id=1, source_target_pairs={{0,4},{4,8},{8,12},{12,14},{14,10},{10,6},{6,2},{2,0},{1,5},{5,9},... | collective-permute-start | bytes 1572872 | tf_op jit(solution)/shard_map/ppermute | solution.py:321
  35.8 18.4 %collective-permute-start.5 = (f32[128,3584]{1,0:T(8,128)S(1)}, f32[128,3584]{1,0:T(8,128)S(1)}, u32[]{:S(2)}, u32[]{:S(2)}) collective-permute-start(f32[128,3584]{1,0:T(8,128)S(1)} %shard_map.75.refs_0_), channel_id=1, source_target_pairs={{0,1},{1,0},{2,3},{3,2},{4,5},{5,4},{6,7},{7,6},{8,9},{9,8},{10,11... | collective-permute-start | bytes 5505032 | tf_op jit(solution)/shard_map/ppermute | solution.py:304
  41.5 6.5 %collective-permute-start.10 = (bf16[64,2048]{1,0:T(8,128)(2,1)S(1)}, bf16[64,2048]{1,0:T(8,128)(2,1)S(1)}, u32[]{:S(2)}, u32[]{:S(2)}) collective-permute-start(bf16[64,2048]{1,0:T(8,128)(2,1)S(1)} %slice.112), channel_id=1, source_target_pairs={{4,0},{8,4},{12,8},{14,12},{10,14},{6,10},{2,6},{0,2},{5,1},{9,5},... | collective-permute-start | bytes 786440 | tf_op jit(solution)/shard_map/ppermute | solution.py:321
  42.1 6.4 %collective-permute-start.9 = (bf16[64,2048]{1,0:T(8,128)(2,1)S(1)}, bf16[64,2048]{1,0:T(8,128)(2,1)S(1)}, u32[]{:S(2)}, u32[]{:S(2)}) collective-permute-start(bf16[64,2048]{1,0:T(8,128)(2,1)S(1)} %slice.111), channel_id=1, source_target_pairs={{0,4},{4,8},{8,12},{12,14},{14,10},{10,6},{6,2},{2,0},{1,5},{5,9},... | collective-permute-start | bytes 786440 | tf_op jit(solution)/shard_map/ppermute | solution.py:321
  51.7 2.5 %collective-permute-start.11 = (f32[64,3584]{1,0:T(8,128)S(1)}, f32[64,3584]{1,0:T(8,128)S(1)}, u32[]{:S(2)}, u32[]{:S(2)}) collective-permute-start(f32[64,3584]{1,0:T(8,128)S(1)} %shard_map.78.refs_0_), channel_id=1, source_target_pairs={{0,1},{1,0},{2,3},{3,2},{4,5},{5,4},{6,7},{7,6},{8,9},{9,8},{10,11... | collective-permute-start | bytes 2752520 | tf_op jit(solution)/shard_map/ppermute | solution.py:304
  51.8 9.6 %collective-permute-start.8 = (f32[128,3584]{1,0:T(8,128)S(1)}, f32[128,3584]{1,0:T(8,128)S(1)}, u32[]{:S(2)}, u32[]{:S(2)}) collective-permute-start(f32[128,3584]{1,0:T(8,128)S(1)} %shard_map.76.refs_0_), channel_id=1, source_target_pairs={{0,1},{1,0},{2,3},{3,2},{4,5},{5,4},{6,7},{7,6},{8,9},{9,8},{10,11... | collective-permute-start | bytes 5505032 | tf_op jit(solution)/shard_map/ppermute | solution.py:304
  56.3 8.3 %collective-permute-start.15 = (bf16[32,2048]{1,0:T(8,128)(2,1)S(1)}, bf16[32,2048]{1,0:T(8,128)(2,1)S(1)}, u32[]{:S(2)}, u32[]{:S(2)}) collective-permute-start(bf16[32,2048]{1,0:T(8,128)(2,1)S(1)} %get-tuple-element.91), channel_id=1, source_target_pairs={{0,4},{4,8},{8,12},{12,14},{14,10},{10,6},{6,2},{2,0},{1,5},{5,9},... | collective-permute-start | bytes 393224 | tf_op jit(solution)/shard_map/ppermute | solution.py:265
  57.9 8.8 %collective-permute-start.14 = (bf16[32,2048]{1,0:T(8,128)(2,1)S(1)}, bf16[32,2048]{1,0:T(8,128)(2,1)S(1)}, u32[]{:S(2)}, u32[]{:S(2)}) collective-permute-start(bf16[32,2048]{1,0:T(8,128)(2,1)S(1)} %get-tuple-element.93), channel_id=1, source_target_pairs={{4,0},{8,4},{12,8},{14,12},{10,14},{6,10},{2,6},{0,2},{5,1},{9,5},... | collective-permute-start | bytes 393224 | tf_op jit(solution)/shard_map/ppermute | solution.py:265
  59.1 8.0 %collective-permute-start.13 = (bf16[32,2048]{1,0:T(8,128)(2,1)S(1)}, bf16[32,2048]{1,0:T(8,128)(2,1)S(1)}, u32[]{:S(2)}, u32[]{:S(2)}) collective-permute-start(bf16[32,2048]{1,0:T(8,128)(2,1)S(1)} %get-tuple-element.92), channel_id=1, source_target_pairs={{0,4},{4,8},{8,12},{12,14},{14,10},{10,6},{6,2},{2,0},{1,5},{5,9},... | collective-permute-start | bytes 393224 | tf_op jit(solution)/shard_map/ppermute | solution.py:265
  61.4 8.1 %collective-permute-start.12 = (bf16[32,2048]{1,0:T(8,128)(2,1)S(1)}, bf16[32,2048]{1,0:T(8,128)(2,1)S(1)}, u32[]{:S(2)}, u32[]{:S(2)}) collective-permute-start(bf16[32,2048]{1,0:T(8,128)(2,1)S(1)} %get-tuple-element.94), channel_id=1, source_target_pairs={{4,0},{8,4},{12,8},{14,12},{10,14},{6,10},{2,6},{0,2},{5,1},{9,5},... | collective-permute-start | bytes 393224 | tf_op jit(solution)/shard_map/ppermute | solution.py:265
  64.6 9.5 %collective-permute-start.19 = (bf16[32,4096]{1,0:T(8,128)(2,1)S(1)}, bf16[32,4096]{1,0:T(8,128)(2,1)S(1)}, u32[]{:S(2)}, u32[]{:S(2)}) collective-permute-start(bf16[32,4096]{1,0:T(8,128)(2,1)S(1)} %pad_maximum_fusion.1), channel_id=1, source_target_pairs={{0,4},{4,8},{8,12},{12,14},{14,10},{10,6},{6,2},{2,0},{1,5},{5,9},... | collective-permute-start | bytes 786440 | tf_op jit(solution)/shard_map/ppermute | solution.py:265
  66.7 9.8 %collective-permute-start.18 = (bf16[32,4096]{1,0:T(8,128)(2,1)S(1)}, bf16[32,4096]{1,0:T(8,128)(2,1)S(1)}, u32[]{:S(2)}, u32[]{:S(2)}) collective-permute-start(bf16[32,4096]{1,0:T(8,128)(2,1)S(1)} %pad_maximum_fusion.2), channel_id=1, source_target_pairs={{4,0},{8,4},{12,8},{14,12},{10,14},{6,10},{2,6},{0,2},{5,1},{9,5},... | collective-permute-start | bytes 786440 | tf_op jit(solution)/shard_map/ppermute | solution.py:265
  67.2 12.6 %collective-permute-start.17 = (bf16[32,4096]{1,0:T(8,128)(2,1)S(1)}, bf16[32,4096]{1,0:T(8,128)(2,1)S(1)}, u32[]{:S(2)}, u32[]{:S(2)}) collective-permute-start(bf16[32,4096]{1,0:T(8,128)(2,1)S(1)} %pad_maximum_fusion.3), channel_id=1, source_target_pairs={{0,4},{4,8},{8,12},{12,14},{14,10},{10,6},{6,2},{2,0},{1,5},{5,9},... | collective-permute-start | bytes 786440 | tf_op jit(solution)/shard_map/ppermute | solution.py:265
  69.5 12.6 %collective-permute-start.16 = (bf16[32,4096]{1,0:T(8,128)(2,1)S(1)}, bf16[32,4096]{1,0:T(8,128)(2,1)S(1)}, u32[]{:S(2)}, u32[]{:S(2)}) collective-permute-start(bf16[32,4096]{1,0:T(8,128)(2,1)S(1)} %pad_maximum_fusion.4), channel_id=1, source_target_pairs={{4,0},{8,4},{12,8},{14,12},{10,14},{6,10},{2,6},{0,2},{5,1},{9,5},... | collective-permute-start | bytes 786440 | tf_op jit(solution)/shard_map/ppermute | solution.py:265
  74.2 12.1 %collective-permute-start.20 = (bf16[32,4096]{1,0:T(8,128)(2,1)S(1)}, bf16[32,4096]{1,0:T(8,128)(2,1)S(1)}, u32[]{:S(2)}, u32[]{:S(2)}) collective-permute-start(bf16[32,4096]{1,0:T(8,128)(2,1)S(1)} %fusion.8), channel_id=1, source_target_pairs={{0,4},{4,8},{8,12},{12,14},{14,10},{10,6},{6,2},{2,0},{1,5},{5,9},... | collective-permute-start | bytes 786440 | tf_op jit(solution)/shard_map/ppermute | solution.py:265
  76.6 11.8 %collective-permute-start.22 = (bf16[32,4096]{1,0:T(8,128)(2,1)S(1)}, bf16[32,4096]{1,0:T(8,128)(2,1)S(1)}, u32[]{:S(2)}, u32[]{:S(2)}) collective-permute-start(bf16[32,4096]{1,0:T(8,128)(2,1)S(1)} %fusion.9), channel_id=1, source_target_pairs={{4,0},{8,4},{12,8},{14,12},{10,14},{6,10},{2,6},{0,2},{5,1},{9,5},... | collective-permute-start | bytes 786440 | tf_op jit(solution)/shard_map/ppermute | solution.py:265
  79.8 11.2 %collective-permute-start.25 = (bf16[32,4096]{1,0:T(8,128)(2,1)S(1)}, bf16[32,4096]{1,0:T(8,128)(2,1)S(1)}, u32[]{:S(2)}, u32[]{:S(2)}) collective-permute-start(bf16[32,4096]{1,0:T(8,128)(2,1)S(1)} %fusion.10), channel_id=1, source_target_pairs={{0,4},{4,8},{8,12},{12,14},{14,10},{10,6},{6,2},{2,0},{1,5},{5,9},... | collective-permute-start | bytes 786440 | tf_op jit(solution)/shard_map/ppermute | solution.py:265
  82.2 11.2 %collective-permute-start.24 = (bf16[32,4096]{1,0:T(8,128)(2,1)S(1)}, bf16[32,4096]{1,0:T(8,128)(2,1)S(1)}, u32[]{:S(2)}, u32[]{:S(2)}) collective-permute-start(bf16[32,4096]{1,0:T(8,128)(2,1)S(1)} %fusion.11), channel_id=1, source_target_pairs={{4,0},{8,4},{12,8},{14,12},{10,14},{6,10},{2,6},{0,2},{5,1},{9,5},... | collective-permute-start | bytes 786440 | tf_op jit(solution)/shard_map/ppermute | solution.py:265
  86.4 12.7 %collective-permute-start.21 = (bf16[32,4096]{1,0:T(8,128)(2,1)S(1)}, bf16[32,4096]{1,0:T(8,128)(2,1)S(1)}, u32[]{:S(2)}, u32[]{:S(2)}) collective-permute-start(bf16[32,4096]{1,0:T(8,128)(2,1)S(1)} %fusion.5), channel_id=1, source_target_pairs={{0,4},{4,8},{8,12},{12,14},{14,10},{10,6},{6,2},{2,0},{1,5},{5,9},... | collective-permute-start | bytes 786440 | tf_op jit(solution)/shard_map/ppermute | solution.py:265
  88.5 10.6 %collective-permute-start.23 = (bf16[32,4096]{1,0:T(8,128)(2,1)S(1)}, bf16[32,4096]{1,0:T(8,128)(2,1)S(1)}, u32[]{:S(2)}, u32[]{:S(2)}) collective-permute-start(bf16[32,4096]{1,0:T(8,128)(2,1)S(1)} %fusion.4), channel_id=1, source_target_pairs={{4,0},{8,4},{12,8},{14,12},{10,14},{6,10},{2,6},{0,2},{5,1},{9,5},... | collective-permute-start | bytes 786440 | tf_op jit(solution)/shard_map/ppermute | solution.py:265
  91.0 11.7 %collective-permute-start.26 = (bf16[32,4096]{1,0:T(8,128)(2,1)S(1)}, bf16[32,4096]{1,0:T(8,128)(2,1)S(1)}, u32[]{:S(2)}, u32[]{:S(2)}) collective-permute-start(bf16[32,4096]{1,0:T(8,128)(2,1)S(1)} %fusion.2), channel_id=1, source_target_pairs={{0,4},{4,8},{8,12},{12,14},{14,10},{10,6},{6,2},{2,0},{1,5},{5,9},... | collective-permute-start | bytes 786440 | tf_op jit(solution)/shard_map/ppermute | solution.py:265
  93.5 9.2 %collective-permute-start.27 = (bf16[32,4096]{1,0:T(8,128)(2,1)S(1)}, bf16[32,4096]{1,0:T(8,128)(2,1)S(1)}, u32[]{:S(2)}, u32[]{:S(2)}) collective-permute-start(bf16[32,4096]{1,0:T(8,128)(2,1)S(1)} %fusion.3), channel_id=1, source_target_pairs={{4,0},{8,4},{12,8},{14,12},{10,14},{6,10},{2,6},{0,2},{5,1},{9,5},... | collective-permute-start | bytes 786440 | tf_op jit(solution)/shard_map/ppermute | solution.py:265
